TPU v7x, 256 devices: a whole 4x4x8 slice. The times are simulated.
256 devices in a mesh: aux: 16 (over x, y), orb: 16 (over z, core).
Axes of the slice: x: 4, y: 4, z: 8, core: 2. Of those that a mesh axis runs over, the one named last changes fastest.
Arguments:
- integrals: bfloat16 [6144, 64, 256], P(('aux', 'orb')), may hold values from -0.375 to 0.375
- coefficients: bfloat16 [160, 64, 512], P('orb'), may hold values from -0.29882812 to 0.29882812
- pair_list: int32 [6144], P(('aux', 'orb')), may hold values from 0 to 159, as said below
- partial_owner: int32 [7680, 1], P(('aux', 'orb')), may hold values from 0 to 15; in each aligned block of 30 rows (0 to 29, 30 to 59, ...) at most 8 rows name the same one
- partial_slot: int32 [7680], P(('aux', 'orb')), may hold values from 0 to 15
Outputs:
- exchange_blocks: float32 [256, 4096], P(('aux', 'orb'))
Inputs may be any that keep to these rules, and one draw needn't show every extreme that they name: `pair_list`: entries 4 s to 4 s + 3 of a device's 24 belong to its local block s: the first two are different blocks of the range o * 10 to (o + 1) * 10 - 1 of its own orb index o, the last two are different blocks of the range of one other orb index, and the 6 local blocks of a device use 6 different other orb indices. `partial_owner`: among the 30 partial blocks of one device no aux index is named more than 8 times, and some device names one exactly 8 times.
All inputs are finite; a program needn't handle non-finite values.
Results may differ from a plain program's by a relative error of at most 0.0039.
Values may be sent and summed in bfloat16 or wider, within the bound.
A program may use at most 64 MiB of HBM per device.

v0:
```python
import jax
import jax.numpy as jnp
import numpy as np
from jax import lax
from jax.sharding import PartitionSpec as P

KB_DEV = 1


def slot_pairs(count):
    table = np.array(
        [
            [row_slot, col_slot]
            for row_slot in range(count)
            for col_slot in range(count)
            if row_slot != col_slot
        ],
        dtype=np.int32,
    )
    return (table[:, 0], table[:, 1])


def shards(integrals, coefficients, pair_list, partial_owner, partial_slot):
    block_size = coefficients.shape[1]
    occ_width = coefficients.shape[2]
    orb_count = lax.axis_size("orb")
    aux_count = lax.axis_size("aux")
    slot_count = pair_list.shape[0] // 4
    aux_functions = integrals.shape[2] // block_size
    everything = lax.all_gather(coefficients, "orb", axis=0, tiled=True)
    selected = everything[pair_list].reshape(slot_count, 4 * block_size, occ_width)
    integral_rows = integrals.reshape(slot_count, 4 * block_size, integrals.shape[2])
    halfway = jnp.einsum(
        "sla,sli->sai", integral_rows, selected, preferred_element_type=jnp.float32
    ).astype(jnp.bfloat16)
    halfway = halfway.reshape(slot_count, block_size, aux_functions, occ_width)
    products = jnp.einsum("smpi,tnpi->stmn", halfway, halfway, preferred_element_type=jnp.float32)
    left_slots, right_slots = slot_pairs(slot_count)
    partial_value = products[left_slots, right_slots].reshape(-1, block_size * block_size)
    owners = partial_owner[:, 0]
    owner_span = KB_DEV * orb_count
    dense_rows = jnp.zeros((owner_span * aux_count, block_size * block_size), jnp.float32)
    dense_rows = dense_rows.at[owners * owner_span + partial_slot].add(partial_value)
    result = lax.psum_scatter(dense_rows, ("aux", "orb"), scatter_dimension=0, tiled=True)
    return result


def solution(mesh):
    in_specs = (
        P(("aux", "orb"), None, None),
        P("orb", None, None),
        P(("aux", "orb")),
        P(("aux", "orb"), None),
        P(("aux", "orb")),
    )
    out_specs = P(("aux", "orb"), None)
    return jax.shard_map(shards, mesh=mesh, in_specs=in_specs, out_specs=out_specs, check_vma=False)
```

profile of v0, /device:TPU:1, one launch (start us, length us, event | category | flops | bytes accessed | tf_op | source)
XLA Modules:
  0.0 370.9 jit_solution(5807444801323718349)
XLA Ops:
  6.5 0.0 copy-start
  6.5 0.0 all-gather.2.cloned.1.call-start
  6.5 0.7 all-gather.2.cloned.1.call-update
  7.3 0.0 all-reduce.3.cloned.1.call-start
  7.3 0.7 compare_select_fusion
  8.0 0.7 compare_select_fusion.1
  8.6 70.6 %all-gather.2.cloned.1.call-done = bf16[160,64,512]{2,1,0:T(8,128)(2,1)} async-done(((bf16[10,64,512]{2,1,0:T(8,128)(2,1)}), bf16[160,64,512]{2,1,0:T(8,128)(2,1)}) %all-gather.2.cloned.1.call-update) | async-done | bytes 10485776 | tf_op jit(solution)/shard_map/all_gather | solution.py:30
  79.2 5.8 %gather_fusion = bf16[24,64,512]{2,1,0:T(8,128)(2,1)} fusion(bf16[160,64,512]{2,1,0:T(8,128)(2,1)} %all-gather.2.cloned.1.call-done, s32[1024]{0:T(1024)S(1)} %pad_clamp_fusion), kind=kCustom, calls=%fused_computation | custom fusion | bytes 3145824 | tf_op jit(solution)/shard_map/gather | solution.py:31
  85.1 0.0 copy-done
  85.1 2.0 fusion.6
  87.1 1.9 reshape.16
  89.0 0.0 copy-start.1
  89.0 3.5 fusion.7
  92.5 0.0 copy-done.1
  92.5 0.7 gather_fusion.1
  93.2 0.3 copy.20
  93.5 0.4 reshape.36
  93.9 3.4 scatter_custom_fusion
  97.3 0.0 all-reduce.3.cloned.1.call-update
  97.3 265.2 %all-reduce.3.cloned.1.call-done = f32[256,4096]{1,0:T(8,128)} async-done(((f32[256,4096]{1,0:T(8,128)}), f32[256,4096]{1,0:T(8,128)}) %all-reduce.3.cloned.1.call-update) | async-done | bytes 4194320
  362.5 1.5 constant_dynamic-slice_fusion
  (1 shorter events, 0.0 us)
Async XLA Ops:
  6.5 78.5 %copy-start = (bf16[24,64,256]{2,1,0:T(8,128)(2,1)S(1)}, bf16[24,64,256]{2,1,0:T(8,128)(2,1)}, u32[]{:S(2)}) copy-start(bf16[24,64,256]{2,1,0:T(8,128)(2,1)} %param.9) | copy-start | bytes 2359300
  6.5 72.7 %all-gather.2.cloned.1.call-start = ((), (), s32[]{:S(2)}) async-start(), calls=%async_computation | async-start | bytes 11141120 | tf_op jit(solution)/shard_map/all_gather | solution.py:30
  7.3 355.3 %all-reduce.3.cloned.1.call-start = ((), (), s32[]{:S(2)}) async-start(), calls=%async_computation.1 | async-start | bytes 8388608
  89.0 3.5 copy-start.1
Sparse Core Ops, SparseCore 0:
  9.2 69.9 all-gather.1
  97.4 265.0 all-reduce.2
where the time goes:
time: 372 us; the launch traced here: 371 us
  waiting for transfers between devices  337 us (91%)
  between operations  13.4 us (4%)
  local copies, waits for them, and re-layouts  10.6 us (3%)
  matrix products  5.55 us (1%)
  other arithmetic  4.74 us (1%)
    unnamed x3, waiting for transfers between devices  266 us
    all_gather x1, waiting for transfers between devices, shards(): everything = lax.all_gather(coefficients, 'orb', axis=0, tiled=True)  70.6 us
  transfers between devices with their start and end apart: 2, of which 2 were waited for; matrix products, arithmetic and copies ran while one was open for 0% of the time, Pallas kernels for 0%

commit v1 on v0

v1 whole, which is shorter than its diff:
```python
import functools

import jax
import jax.numpy as jnp
from jax import lax
from jax.experimental import pallas as pl
from jax.experimental.pallas import tpu as pltpu
from jax.sharding import PartitionSpec as P

MESH = pl.DeviceIdType.MESH
F32, BF16, I32 = jnp.float32, jnp.bfloat16, jnp.int32


def kernel(
    dims,
    ints_ref,
    coef_ref,
    pairs_ref,
    owner_ref,
    slot_ref,
    out_ref,
    gbuf,
    cbuf,
    zbuf,
    msgs,
    idsm,
    packed,
    sel,
    gt,
    hcat,
    xbuf,
    xsend,
    xrecv,
    onehot,
    dsend,
    drecv,
    fsend,
    frecv,
    load_sem,
    zs_sem,
    zr_sem,
    ws_sem,
    wr_sem,
    is_sem,
    ir_sem,
    ps_sem,
    pr_sem,
    xs_sem,
    xr_sem,
    ds_sem,
    dr_sem,
    fs_sem,
    fr_sem,
):
    na, no, lmb, bs, nocc, naux, per = dims
    nz = no // 2
    nic = nocc // 128
    mp = bs // na // 2
    half = lmb // 2
    width = na * 16
    rows = na * no
    el = mp * 128
    a = lax.axis_index("aux")
    o = lax.axis_index("orb")
    z, c = o // 2, o % 2
    sib = o + 1 - 2 * c
    lg = pl.multiple_of((a // nic) * 16, 16)
    lane0 = pl.multiple_of((a % nic) * 128, 128)
    ic = a % nic

    load_c = pltpu.make_async_copy(coef_ref, cbuf, load_sem.at[0])
    load_g = pltpu.make_async_copy(ints_ref, gbuf, load_sem.at[1])
    load_c.start()
    load_g.start()

    barrier = pltpu.get_barrier_semaphore()

    def greet_aux(i, _):
        pl.semaphore_signal(barrier, inc=1, device_id=((a + i) % na, o), device_id_type=MESH)
        return 0

    def greet_orb(i, _):
        pl.semaphore_signal(barrier, inc=1, device_id=(a, (o + i) % no), device_id_type=MESH)
        return 0

    lax.fori_loop(1, no, greet_orb, 0)
    lax.fori_loop(1, na, greet_aux, 0)

    row_at = lax.broadcasted_iota(I32, (8, width), 0)
    lane_at = lax.broadcasted_iota(I32, (8, width), 1)
    note = jnp.zeros((8, width), I32)
    for s in range(lmb):
        for t in range(lmb):
            if s != t:
                j = s * (lmb - 1) + t - (1 if t > s else 0)
                place = slot_ref[j] * na + owner_ref[j] + 1
                here = (row_at == t) & ((lane_at == a * 16 + s) | (lane_at == a * 16 + 8 + s))
                note = jnp.where(here, place, note)
    for j in range(4 * lmb):
        note = jnp.where((row_at == lmb) & (lane_at == j), pairs_ref[j], note)
    msgs[a] = note

    pl.semaphore_wait(barrier, na + no - 2)
    load_c.wait()

    tiles = cbuf.at[:, pl.ds(lg, 16), pl.ds(lane0, 128)]
    mine = pltpu.make_async_copy(tiles, zbuf.at[pl.ds(o * per, per)], load_sem.at[2])

    def z_copy(i):
        return pltpu.make_async_remote_copy(
            src_ref=tiles,
            dst_ref=zbuf.at[pl.ds(o * per, per)],
            send_sem=zs_sem.at[i],
            recv_sem=zr_sem.at[z],
            device_id=(a, ((z + i) % nz) * 2 + c),
            device_id_type=MESH,
        )

    def z_arrival(i):
        src = (z + i) % nz
        part = zbuf.at[pl.ds((src * 2 + c) * per, per)]
        return pltpu.make_async_remote_copy(
            src_ref=part,
            dst_ref=part,
            send_sem=zs_sem.at[i],
            recv_sem=zr_sem.at[src],
            device_id=(a, sib),
            device_id_type=MESH,
        )

    def own_swap():
        return pltpu.make_async_remote_copy(
            src_ref=tiles,
            dst_ref=zbuf.at[pl.ds(o * per, per)],
            send_sem=ws_sem.at[z],
            recv_sem=wr_sem.at[z],
            device_id=(a, sib),
            device_id_type=MESH,
        )

    def swap_copy(i):
        src = (z + i) % nz
        part = zbuf.at[pl.ds((src * 2 + c) * per, per)]
        return pltpu.make_async_remote_copy(
            src_ref=part,
            dst_ref=part,
            send_sem=ws_sem.at[src],
            recv_sem=wr_sem.at[src],
            device_id=(a, sib),
            device_id_type=MESH,
        )

    def swap_arrival(i):
        src = (z + i) % nz
        part = zbuf.at[pl.ds((src * 2 + 1 - c) * per, per)]
        return pltpu.make_async_remote_copy(
            src_ref=part,
            dst_ref=part,
            send_sem=ws_sem.at[src],
            recv_sem=wr_sem.at[src],
            device_id=(a, sib),
            device_id_type=MESH,
        )

    def start_z(i, _):
        z_copy(i).start()
        return 0

    lax.fori_loop(1, nz, start_z, 0)
    own_swap().start()
    mine.start()

    def id_copy(i):
        return pltpu.make_async_remote_copy(
            src_ref=msgs.at[a],
            dst_ref=msgs.at[a],
            send_sem=is_sem.at[i],
            recv_sem=ir_sem.at[a],
            device_id=((a + i) % na, o),
            device_id_type=MESH,
        )

    def id_arrival(i):
        src = (a + i) % na
        return pltpu.make_async_remote_copy(
            src_ref=msgs.at[src],
            dst_ref=msgs.at[src],
            send_sem=is_sem.at[i],
            recv_sem=ir_sem.at[src],
            device_id=(src, o),
            device_id_type=MESH,
        )

    def start_ids(i, _):
        id_copy(i).start()
        return 0

    lax.fori_loop(1, na, start_ids, 0)

    for s in range(lmb):
        for k in range(2):
            block = cbuf[lax.rem(pairs_ref[4 * s + k], per)]
            for i in range(nic):
                sel[i, s, k] = block[:, i * 128 : (i + 1) * 128]

    load_g.wait()
    height = bs * naux
    r_at = lax.broadcasted_iota(I32, (height, height), 0)
    c_at = lax.broadcasted_iota(I32, (height, height), 1)
    turn = (c_at == (r_at % bs) * naux + r_at // bs).astype(F32).astype(BF16)
    for s in range(lmb):
        block = gbuf[4 * s : 4 * s + 4].reshape(4 * bs, height)
        gt[s] = lax.dot_general(turn, block, (((1,), (1,)), ((), ())), preferred_element_type=F32).astype(BF16)
    xbuf[...] = jnp.zeros_like(xbuf)

    def wait_ids(i, _):
        id_arrival(i).wait_recv()
        return 0

    lax.fori_loop(1, na, wait_ids, 0)
    to_scalar = pltpu.make_async_copy(msgs.at[:, :, pl.ds(0, min(width, 128))], idsm, load_sem.at[3])
    to_scalar.start()

    ids = msgs[0]
    for src in range(1, na):
        ids = ids + msgs[src]
    r_at = lax.broadcasted_iota(I32, (rows, width), 0) + 1
    l_at = (lax.broadcasted_iota(I32, (rows, width), 1) // 8) % 2
    for h in range(2):
        for tp in range(half):
            hit = r_at == ids[2 * tp + h : 2 * tp + h + 1, :]
            for m2 in range(2):
                onehot[pl.ds((m2 * 2 + h) * rows, rows), pl.ds(tp * width, width)] = (
                    jnp.where(hit & (l_at == m2), 1.0, 0.0).astype(BF16)
                )
    to_scalar.wait()

    def forward(i, _):
        z_arrival(i).wait_recv()
        swap_copy(i).start()
        return 0

    lax.fori_loop(1, nz, forward, 0)
    mine.wait()

    def wait_swap(i, _):
        swap_arrival(i).wait_recv()
        return 0

    lax.fori_loop(0, nz, wait_swap, 0)

    def pack_copy(i):
        to = (a + i) % na
        return pltpu.make_async_remote_copy(
            src_ref=packed.at[to],
            dst_ref=sel.at[ic, :, pl.ds(2, 2), pl.ds(lg, 16), :],
            send_sem=ps_sem.at[i],
            recv_sem=pr_sem.at[a],
            device_id=(to, o),
            device_id_type=MESH,
        )

    def pack_arrival(i):
        src = (a + i) % na
        return pltpu.make_async_remote_copy(
            src_ref=packed.at[src],
            dst_ref=sel.at[src % nic, :, pl.ds(2, 2), pl.ds(pl.multiple_of((src // nic) * 16, 16), 16), :],
            send_sem=ps_sem.at[i],
            recv_sem=pr_sem.at[src],
            device_id=(src, o),
            device_id_type=MESH,
        )

    def pack(i, _):
        to = (a + i) % na
        for s in range(lmb):
            for k in range(2):
                packed[to, s, k] = zbuf[idsm[to, lmb, 4 * s + 2 + k]]
        pack_copy(i).start()
        return 0

    lax.fori_loop(1, na, pack, 0)
    for s in range(lmb):
        for k in range(2):
            sel[ic, s, 2 + k, pl.ds(lg, 16), :] = zbuf[pairs_ref[4 * s + 2 + k]]

    def wait_pack(i, _):
        pack_arrival(i).wait_recv()
        return 0

    lax.fori_loop(1, na, wait_pack, 0)

    for s in range(lmb):
        block = jnp.concatenate([sel[i, s].reshape(4 * bs, 128) for i in range(nic)], axis=1)
        halfway = jnp.dot(gt[s], block, preferred_element_type=F32).astype(BF16)
        for p in range(naux):
            hcat[pl.ds(s * bs, bs), pl.ds(p * nocc, nocc)] = halfway[p * bs : (p + 1) * bs]

    whole = hcat[...]
    for s in range(lmb):
        part = lax.dot_general(
            hcat[pl.ds(s * bs, bs), :], whole, (((1,), (1,)), ((), ())), preferred_element_type=F32
        )
        for tp in range(half):
            xbuf[tp, pl.ds(s, bs, stride=8), :] = part[:, tp * 128 : (tp + 1) * 128]

    def x_copy(i):
        to = (a + i) % na
        return pltpu.make_async_remote_copy(
            src_ref=xsend.at[to],
            dst_ref=xrecv.at[:, a],
            send_sem=xs_sem.at[i],
            recv_sem=xr_sem.at[a],
            device_id=(to, o),
            device_id_type=MESH,
        )

    def x_arrival(i):
        src = (a + i) % na
        return pltpu.make_async_remote_copy(
            src_ref=xsend.at[src],
            dst_ref=xrecv.at[:, src],
            send_sem=xs_sem.at[i],
            recv_sem=xr_sem.at[src],
            device_id=(src, o),
            device_id_type=MESH,
        )

    def x_rows(e, q):
        at = pl.ds(pl.multiple_of((e * mp + q) * 16, 16), 16)
        return jnp.concatenate([xbuf[tp, at, :] for tp in range(half)], axis=1).astype(BF16)

    def send_x(i, _):
        to = (a + i) % na
        for q in range(mp):
            xsend[to, q] = x_rows(to, q)
        x_copy(i).start()
        return 0

    lax.fori_loop(1, na, send_x, 0)
    for q in range(mp):
        xrecv[q, a] = x_rows(a, q)

    def wait_x(i, _):
        x_arrival(i).wait_recv()
        return 0

    lax.fori_loop(1, na, wait_x, 0)

    right = [
        jnp.concatenate(
            [xrecv[q, :, :, pl.ds(tp * 128, 128)].reshape(width, 128) for q in range(mp)], axis=1
        )
        for tp in range(half)
    ]

    def product(block):
        total = None
        for tp in range(half):
            term = jnp.dot(
                onehot[pl.ds(block * rows, rows), pl.ds(tp * width, width)], right[tp], preferred_element_type=F32
            )
            total = term if total is None else total + term
        return total

    z00, z01, z10, z11 = product(0), product(1), product(2), product(3)
    low = lax.broadcasted_iota(I32, (rows, 128), 1) < 64
    for q in range(mp):
        at = slice(q * 128, (q + 1) * 128)
        first = z00[:, at] + pltpu.roll(z01[:, at], 64, 1)
        second = pltpu.roll(z10[:, at], 64, 1) + z11[:, at]
        dense = jnp.where(low, first, second).astype(BF16)
        dsend[:, :, pl.ds(q * 128, 128)] = dense.reshape(no, na, 128)

    def d_copy(i):
        to = (o + i) % no
        return pltpu.make_async_remote_copy(
            src_ref=dsend.at[to],
            dst_ref=drecv.at[o],
            send_sem=ds_sem.at[i],
            recv_sem=dr_sem.at[o],
            device_id=(a, to),
            device_id_type=MESH,
        )

    def d_arrival(i):
        src = (o + i) % no
        return pltpu.make_async_remote_copy(
            src_ref=dsend.at[src],
            dst_ref=drecv.at[src],
            send_sem=ds_sem.at[i],
            recv_sem=dr_sem.at[src],
            device_id=(a, src),
            device_id_type=MESH,
        )

    def send_d(i, _):
        d_copy(i).start()
        return 0

    lax.fori_loop(1, no, send_d, 0)
    drecv[o] = dsend[o]

    def wait_d(i, _):
        d_arrival(i).wait_recv()
        return 0

    lax.fori_loop(1, no, wait_d, 0)

    total = drecv[0].astype(F32)
    for src in range(1, no):
        total = total + drecv[src].astype(F32)
    for r in range(na):
        fsend[r] = total[r : r + 1, :]

    def f_copy(i):
        to = (a + i) % na
        return pltpu.make_async_remote_copy(
            src_ref=fsend.at[to],
            dst_ref=frecv.at[a],
            send_sem=fs_sem.at[i],
            recv_sem=fr_sem.at[a],
            device_id=(to, o),
            device_id_type=MESH,
        )

    def f_arrival(i):
        src = (a + i) % na
        return pltpu.make_async_remote_copy(
            src_ref=fsend.at[src],
            dst_ref=frecv.at[src],
            send_sem=fs_sem.at[i],
            recv_sem=fr_sem.at[src],
            device_id=(src, o),
            device_id_type=MESH,
        )

    def send_f(i, _):
        f_copy(i).start()
        return 0

    lax.fori_loop(1, na, send_f, 0)
    frecv[a] = fsend[a]

    def settle_aux(i, _):
        id_copy(i).wait_send()
        pack_copy(i).wait_send()
        x_copy(i).wait_send()
        return 0

    def settle_z(i, _):
        z_copy(i).wait_send()
        swap_copy(i).wait_send()
        return 0

    def settle_d(i, _):
        d_copy(i).wait_send()
        return 0

    lax.fori_loop(1, na, settle_aux, 0)
    lax.fori_loop(1, nz, settle_z, 0)
    own_swap().wait_send()
    lax.fori_loop(1, no, settle_d, 0)

    def wait_f(i, _):
        f_arrival(i).wait_recv()
        f_copy(i).wait_send()
        return 0

    lax.fori_loop(1, na, wait_f, 0)
    for e in range(na):
        out_ref[:, pl.ds(e * el, el)] = frecv[e]


def shards(integrals, coefficients, pair_list, partial_owner, partial_slot):
    na, no = lax.axis_size("aux"), lax.axis_size("orb")
    per, bs, nocc = coefficients.shape
    lmb = pair_list.shape[0] // 4
    naux = integrals.shape[2] // bs
    mp = bs // na // 2
    width = na * 16
    rows = na * no
    el = mp * 128
    nz = no // 2
    dims = (na, no, lmb, bs, nocc, naux, per)
    dma = pltpu.SemaphoreType.DMA
    vmem = pltpu.VMEM
    any_spec = pl.BlockSpec(memory_space=pltpu.HBM)
    smem_spec = pl.BlockSpec(memory_space=pltpu.SMEM)
    return pl.pallas_call(
        functools.partial(kernel, dims),
        out_shape=jax.ShapeDtypeStruct((1, bs * bs), F32),
        in_specs=[any_spec, any_spec, smem_spec, smem_spec, smem_spec],
        out_specs=pl.BlockSpec(memory_space=pltpu.VMEM),
        scratch_shapes=[
            vmem(integrals.shape, BF16),
            vmem(coefficients.shape, BF16),
            vmem((no * per, 16, 128), BF16),
            vmem((na, 8, width), I32),
            pltpu.SMEM((na, 8, min(width, 128)), I32),
            vmem((na, lmb, 2, 16, 128), BF16),
            vmem((nocc // 128, lmb, 4, bs, 128), BF16),
            vmem((lmb, bs * naux, 4 * bs), BF16),
            vmem((lmb * bs, naux * nocc), BF16),
            vmem((lmb // 2, bs * 8, 128), F32),
            vmem((na, mp, 16, lmb * bs), BF16),
            vmem((mp, na, 16, lmb * bs), BF16),
            vmem((4 * rows, lmb // 2 * width), BF16),
            vmem((no, na, el), BF16),
            vmem((no, na, el), BF16),
            vmem((na, 1, el), F32),
            vmem((na, 1, el), F32),
            dma((4,)),
            dma((nz,)),
            dma((nz,)),
            dma((nz,)),
            dma((nz,)),
            dma((na,)),
            dma((na,)),
            dma((na,)),
            dma((na,)),
            dma((na,)),
            dma((na,)),
            dma((no,)),
            dma((no,)),
            dma((na,)),
            dma((na,)),
        ],
        compiler_params=pltpu.CompilerParams(
            collective_id=0, has_side_effects=True, vmem_limit_bytes=40 * 2**20
        ),
    )(integrals, coefficients, pair_list, partial_owner.reshape(-1), partial_slot)


def solution(mesh):
    in_specs = (
        P(("aux", "orb"), None, None),
        P("orb", None, None),
        P(("aux", "orb")),
        P(("aux", "orb"), None),
        P(("aux", "orb")),
    )
    out_specs = P(("aux", "orb"), None)
    return jax.shard_map(shards, mesh=mesh, in_specs=in_specs, out_specs=out_specs, check_vma=False)
```

time: 372 us -> 62.1 us (0.17)
  waiting for transfers between devices: 337 us -> 0 us
  Pallas kernels: 0 us -> 58.4 us
  between operations: 13.4 us -> 0.02 us
  local copies, waits for them, and re-layouts: 10.6 us -> 3.51 us
  matrix products: 5.55 us -> 0 us
  other arithmetic: 4.74 us -> 0 us
    unnamed x3 -> x0, waiting for transfers between devices: 266 us -> none
    all_gather x1 -> x0, waiting for transfers between devices: 70.6 us -> none  [shards(): everything = lax.all_gather(coefficients, 'orb', axis=0, tiled=True)]
    pallas_call x0 -> x1, Pallas kernels: none -> 58.4 us  [shards(): pl.pallas_call(functools.partial(kernel, dims), out_shape=jax.ShapeDtypeS...]
    gather x3 -> x0, local copies, waits for them, and re-layouts: 6.86 us -> none  [the longest x1 5.83 us: shards(): everything[pair_list].reshape(slot_count, 4 * block_size, occ_width)]
    dot_general x2 -> x0, matrix products: 5.55 us -> none  [the longest x1 3.52 us: shards(): jnp.einsum('smpi,tnpi->stmn', halfway, halfway, preferred_element_type=jn...]
  transfers between devices with their start and end apart: 2 -> 0, of which waited for: 2 -> 0; matrix products, arithmetic and copies ran while one was open for 0% -> 0% of each run, Pallas kernels for 0% -> 0%
where the time goes in v1:
time: 62.1 us; the launch traced here: 62 us
  Pallas kernels  58.4 us (94%)
  local copies, waits for them, and re-layouts  3.51 us (6%)
    pallas_call x1, Pallas kernels, shards(): pl.pallas_call(functools.partial(kernel, dims), out_shape=jax.ShapeDtypeS...  58.4 us
    unnamed x11, local copies, waits for them, and re-layouts  3.51 us

profile of v1, /device:TPU:1, one launch (start us, length us, event | category | flops | bytes accessed | tf_op | source)
XLA Modules:
  0.0 62.0 jit_solution(14627603852284767460)
XLA Ops:
  0.0 0.0 copy-start.4
  0.0 0.0 copy-start.3
  0.0 0.0 copy-start.2
  0.0 0.6 %copy-done.4 = s32[30]{0:T(128)S(1)} copy-done((s32[30]{0:T(128)S(1)}, s32[30]{0:T(128)}, u32[]{:S(2)}) %copy-start.4) | copy-done | bytes 144
  0.7 0.0 copy-done.3
  0.7 0.0 copy-done.2
  0.7 0.0 copy-start
  0.7 1.1 %copy-done = bf16[24,64,256]{2,1,0:T(8,128)(2,1)S(1)} copy-done((bf16[24,64,256]{2,1,0:T(8,128)(2,1)S(1)}, bf16[24,64,256]{2,1,0:T(8,128)(2,1)}, u32[]{:S(2)}) %copy-start) | copy-done | bytes 786456
  1.8 0.0 copy-start.1
  1.8 1.1 %copy-done.1 = bf16[10,64,512]{2,1,0:T(8,128)(2,1)S(1)} copy-done((bf16[10,64,512]{2,1,0:T(8,128)(2,1)S(1)}, bf16[10,64,512]{2,1,0:T(8,128)(2,1)}, u32[]{:S(2)}) %copy-start.1) | copy-done | bytes 655384
  2.9 58.4 %shard_map.55 = f32[1,4096]{1,0:T(1,128)S(1)} custom-call(bf16[24,64,256]{2,1,0:T(8,128)(2,1)S(1)} %copy-done, bf16[10,64,512]{2,1,0:T(8,128)(2,1)S(1)} %copy-done.1, s32[24]{0:T(128)S(1)} %copy-done.2, s32[30]{0:T(128)S(1)} %bitcast.1, s32[30]{0:T(128)S(1)} %copy-done.4), custom_call_target="tpu_custom_call" | custom-call | tf_op jit(solution)/shard_map/pallas_call | solution.py:490
  61.4 0.6 copy.7
Async XLA Ops:
  0.0 0.7 %copy-start.4 = (s32[30]{0:T(128)S(1)}, s32[30]{0:T(128)}, u32[]{:S(2)}) copy-start(s32[30]{0:T(128)} %slot_ref.1) | copy-start | bytes 364
  0.0 0.7 %copy-start.3 = (s32[30,1]{0,1:T(1,128)S(1)}, s32[30,1]{0,1:T(1,128)}, u32[]{:S(2)}) copy-start(s32[30,1]{0,1:T(1,128)} %param.8) | copy-start | bytes 364
  0.0 0.7 %copy-start.2 = (s32[24]{0:T(128)S(1)}, s32[24]{0:T(128)}, u32[]{:S(2)}) copy-start(s32[24]{0:T(128)} %pairs_ref.1) | copy-start | bytes 292
  0.7 1.1 %copy-start = (bf16[24,64,256]{2,1,0:T(8,128)(2,1)S(1)}, bf16[24,64,256]{2,1,0:T(8,128)(2,1)}, u32[]{:S(2)}) copy-start(bf16[24,64,256]{2,1,0:T(8,128)(2,1)} %ints_ref.1) | copy-start | bytes 2359300
  1.8 1.1 %copy-start.1 = (bf16[10,64,512]{2,1,0:T(8,128)(2,1)S(1)}, bf16[10,64,512]{2,1,0:T(8,128)(2,1)}, u32[]{:S(2)}) copy-start(bf16[10,64,512]{2,1,0:T(8,128)(2,1)} %coef_ref.1) | copy-start | bytes 1966084

commit v2 on v0

v2 whole, which is shorter than its diff:
```python
import functools
import math

import jax
import jax.numpy as jnp
from jax import lax
from jax.experimental import pallas as pl
from jax.experimental.pallas import tpu as pltpu
from jax.sharding import PartitionSpec as P

MESH = pl.DeviceIdType.MESH
F32, BF16, I32 = jnp.float32, jnp.bfloat16, jnp.int32


def kernel(
    dims,
    ints_ref,
    coef_ref,
    pairs_hbm,
    owner_hbm,
    slot_hbm,
    out_ref,
    pairs_ref,
    owner_ref,
    slot_ref,
    gbuf,
    cbuf,
    tiles,
    zbuf_a,
    zbuf_b,
    msgs,
    idsm,
    packed,
    near,
    far,
    gt,
    hcat,
    xbuf,
    xsend,
    xrecv,
    onehot,
    dsend,
    drecv,
    fsend,
    frecv,
    load_sem,
    send_sem,
    recv_sem,
):
    na, no, lmb, bs, nocc, naux, per = dims
    side = math.isqrt(na)
    nz = no // 2
    nic = nocc // 128
    mp = bs // na // 2
    half = lmb // 2
    width = na * 16
    rows = na * no
    el = mp * 128
    a = lax.axis_index("aux")
    o = lax.axis_index("orb")
    x, y = a // side, a % side
    z, c = o // 2, o % 2
    sib = o + 1 - 2 * c
    lg = pl.multiple_of((a // nic) * 16, 16)
    lane0 = pl.multiple_of((a % nic) * 128, 128)
    own = pl.ds(o * per, per)
    zbuf = (zbuf_a, zbuf_b)

    def plane_peer(i):
        turn = na // 2 + side // 2
        j = jnp.where(i < na - turn, i + turn, i - (na - turn) + 1)
        return ((x + j // side) % side) * side + (y + j % side) % side

    z_order = sorted(range(1, nz), key=lambda i: -min(i, nz - i))
    o_order = sorted(range(1, no), key=lambda i: -min(i, no - i))

    barrier = pltpu.get_barrier_semaphore()
    for i in o_order:
        pl.semaphore_signal(barrier, inc=1, device_id=(a, (o + i) % no), device_id_type=MESH)

    def greet(i, _):
        pl.semaphore_signal(barrier, inc=1, device_id=(plane_peer(i), o), device_id_type=MESH)
        return 0

    lax.fori_loop(0, na - 1, greet, 0)

    load_t = pltpu.make_async_copy(coef_ref.at[:, pl.ds(lg, 16), pl.ds(lane0, 128)], tiles, load_sem.at[2])
    load_c = pltpu.make_async_copy(coef_ref, cbuf, load_sem.at[0])
    load_g = pltpu.make_async_copy(ints_ref, gbuf, load_sem.at[1])
    scalars = [
        pltpu.make_async_copy(pairs_hbm, pairs_ref, load_sem.at[4]),
        pltpu.make_async_copy(owner_hbm, owner_ref, load_sem.at[5]),
        pltpu.make_async_copy(slot_hbm, slot_ref, load_sem.at[6]),
    ]
    load_t.start()
    for copy in scalars:
        copy.start()
    load_c.start()
    load_g.start()

    def remote(src, dst, stage, device):
        return pltpu.make_async_remote_copy(
            src_ref=src,
            dst_ref=dst,
            send_sem=send_sem.at[stage],
            recv_sem=recv_sem.at[stage],
            device_id=device,
            device_id_type=MESH,
        )

    def all_of(part, stage):
        return remote(part, part, stage, (a, sib))

    za, zb, wa, wb, ids_at, pa, pb, xs, ds, fs = range(10)

    load_t.wait()
    zbuf_a[own] = tiles[:, 0:8, :]
    zbuf_b[own] = tiles[:, 8:16, :]
    for copy in scalars:
        copy.wait()

    row_at = lax.broadcasted_iota(I32, (8, width), 0)
    lane_at = lax.broadcasted_iota(I32, (8, width), 1)
    note = jnp.zeros((8, width), I32)
    for s in range(lmb):
        for t in range(lmb):
            if s != t:
                j = s * (lmb - 1) + t - (1 if t > s else 0)
                place = slot_ref[j] * na + owner_ref[j] + 1
                here = (row_at == t) & ((lane_at == a * 16 + s) | (lane_at == a * 16 + 8 + s))
                note = jnp.where(here, place, note)
    for j in range(4 * lmb):
        if j % 4 >= 2:
            note = jnp.where((row_at == lmb) & (lane_at == j), pairs_ref[j], note)
    msgs[a] = note

    pl.semaphore_wait(barrier, na + no - 2)

    def start_z(h, stage):
        for i in z_order:
            remote(zbuf[h].at[own], zbuf[h].at[own], stage, (a, ((z + i) % nz) * 2 + c)).start()

    start_z(0, za)

    def start_ids(i, _):
        remote(msgs.at[a], msgs.at[a], ids_at, (plane_peer(i), o)).start()
        return 0

    lax.fori_loop(0, na - 1, start_ids, 0)
    start_z(1, zb)

    load_g.wait()
    height = bs * naux
    r_at = lax.broadcasted_iota(I32, (height, height), 0)
    c_at = lax.broadcasted_iota(I32, (height, height), 1)
    turn = (c_at == (r_at % bs) * naux + r_at // bs).astype(F32).astype(BF16)
    j = c_at - 2 * bs
    source = 2 * bs + (j // 8 % 2) * bs + (j // 16 % (bs // 16)) * 16 + (j // bs) * 8 + j % 8
    order = (r_at == jnp.where(c_at < 2 * bs, c_at, source)).astype(F32).astype(BF16)
    for s in range(lmb):
        block = gbuf[4 * s : 4 * s + 4].reshape(4 * bs, height)
        turned = lax.dot_general(turn, block, (((1,), (1,)), ((), ())), preferred_element_type=F32).astype(BF16)
        gt[s] = jnp.dot(turned, order, preferred_element_type=F32).astype(BF16)

    load_c.wait()
    for s in range(lmb):
        for k in range(2):
            near[s, pl.ds(k * bs, bs), :] = cbuf[lax.rem(pairs_ref[4 * s + k], per)]
    xbuf[...] = jnp.zeros_like(xbuf)

    all_of(msgs.at[pl.ds(0, na - 1)], ids_at).wait_recv()
    to_scalar = pltpu.make_async_copy(msgs.at[:, :, pl.ds(0, min(width, 128))], idsm, load_sem.at[3])
    to_scalar.start()

    ids = msgs[0]
    for src in range(1, na):
        ids = ids + msgs[src]
    to_scalar.wait()

    def swap(h, z_stage, w_stage):
        all_of(zbuf[h].at[pl.ds(0, (nz - 1) * per)], z_stage).wait_recv()
        for i in range(nz):
            part = zbuf[h].at[pl.ds((2 * i + c) * per, per)]
            remote(part, part, w_stage, (a, sib)).start()

    def pair(h, to, s):
        return jnp.concatenate(
            [zbuf[h][idsm[to, lmb, 4 * s + 2]], zbuf[h][idsm[to, lmb, 4 * s + 3]]], axis=0
        )

    def exchange(h, w_stage, p_stage):
        all_of(zbuf[h].at[pl.ds(0, nz * per)], w_stage).wait_recv()

        def pack(i, _):
            to = plane_peer(i)
            for s in range(lmb):
                packed[h, to, s] = pair(h, to, s)
            remote(packed.at[h, to], far.at[h, a], p_stage, (to, o)).start()
            return 0

        lax.fori_loop(0, na - 1, pack, 0)
        for s in range(lmb):
            far[h, a, s] = pair(h, a, s)

    swap(0, za, wa)
    exchange(0, wa, pa)
    swap(1, zb, wb)
    exchange(1, wb, pb)

    r_at = lax.broadcasted_iota(I32, (rows, width), 0) + 1
    l_at = (lax.broadcasted_iota(I32, (rows, width), 1) // 8) % 2
    for h in range(2):
        for tp in range(half):
            hit = r_at == ids[2 * tp + h : 2 * tp + h + 1, :]
            for m2 in range(2):
                onehot[pl.ds((m2 * 2 + h) * rows, rows), pl.ds(tp * width, width)] = (
                    jnp.where(hit & (l_at == m2), 1.0, 0.0).astype(BF16)
                )

    all_of(far.at[0, pl.ds(0, na - 1)], pa).wait_recv()
    all_of(far.at[1, pl.ds(0, na - 1)], pb).wait_recv()

    for s in range(lmb):
        there = [
            jnp.concatenate([far[h, g * nic + i, s] for h in range(2) for g in range(bs // 16)], axis=0)
            for i in range(nic)
        ]
        block = jnp.concatenate([near[s], jnp.concatenate(there, axis=1)], axis=0)
        halfway = jnp.dot(gt[s], block, preferred_element_type=F32).astype(BF16)
        for p in range(naux):
            hcat[pl.ds(s * bs, bs), pl.ds(p * nocc, nocc)] = halfway[p * bs : (p + 1) * bs]

    whole = hcat[...]
    products = lax.dot_general(whole, whole, (((1,), (1,)), ((), ())), preferred_element_type=F32)
    for s in range(lmb):
        for tp in range(half):
            xbuf[tp, pl.ds(s, bs, stride=8), :] = products[s * bs : (s + 1) * bs, tp * 128 : (tp + 1) * 128]

    def x_rows(e, q):
        at = pl.ds(pl.multiple_of((e * mp + q) * 16, 16), 16)
        return jnp.concatenate([xbuf[tp, at, :] for tp in range(half)], axis=1).astype(BF16)

    def send_x(i, _):
        to = plane_peer(i)
        for q in range(mp):
            xsend[to, q] = x_rows(to, q)
        remote(xsend.at[to], xrecv.at[a], xs, (to, o)).start()
        return 0

    lax.fori_loop(0, na - 1, send_x, 0)
    for q in range(mp):
        xrecv[a, q] = x_rows(a, q)
    all_of(xrecv.at[pl.ds(0, na - 1)], xs).wait_recv()

    right = [
        jnp.concatenate(
            [xrecv[:, q, :, pl.ds(tp * 128, 128)].reshape(width, 128) for q in range(mp)], axis=1
        )
        for tp in range(half)
    ]

    def product(block):
        total = None
        for tp in range(half):
            term = jnp.dot(
                onehot[pl.ds(block * rows, rows), pl.ds(tp * width, width)], right[tp], preferred_element_type=F32
            )
            total = term if total is None else total + term
        return total

    z00, z01, z10, z11 = product(0), product(1), product(2), product(3)
    low = lax.broadcasted_iota(I32, (rows, 128), 1) < 64
    for q in range(mp):
        at = slice(q * 128, (q + 1) * 128)
        first = z00[:, at] + pltpu.roll(z01[:, at], 64, 1)
        second = pltpu.roll(z10[:, at], 64, 1) + z11[:, at]
        dense = jnp.where(low, first, second).astype(BF16)
        dsend[:, :, pl.ds(q * 128, 128)] = dense.reshape(no, na, 128)

    for i in o_order:
        to = (o + i) % no
        remote(dsend.at[to], drecv.at[o], ds, (a, to)).start()
    drecv[o] = dsend[o]
    all_of(drecv.at[pl.ds(0, no - 1)], ds).wait_recv()

    total = drecv[0].astype(F32)
    for src in range(1, no):
        total = total + drecv[src].astype(F32)
    for r in range(na):
        fsend[r] = total[r : r + 1, :]

    def send_f(i, _):
        to = plane_peer(i)
        remote(fsend.at[to], frecv.at[a], fs, (to, o)).start()
        return 0

    lax.fori_loop(0, na - 1, send_f, 0)
    frecv[a] = fsend[a]

    for h, (z_stage, w_stage, p_stage) in enumerate(((za, wa, pa), (zb, wb, pb))):
        all_of(zbuf[h].at[pl.ds(0, (nz - 1) * per)], z_stage).wait_send()
        all_of(zbuf[h].at[pl.ds(0, nz * per)], w_stage).wait_send()
        all_of(packed.at[h, pl.ds(0, na - 1)], p_stage).wait_send()
    all_of(msgs.at[pl.ds(0, na - 1)], ids_at).wait_send()
    all_of(xsend.at[pl.ds(0, na - 1)], xs).wait_send()
    all_of(dsend.at[pl.ds(0, no - 1)], ds).wait_send()
    all_of(frecv.at[pl.ds(0, na - 1)], fs).wait_recv()
    all_of(fsend.at[pl.ds(0, na - 1)], fs).wait_send()
    for e in range(na):
        out_ref[:, pl.ds(e * el, el)] = frecv[e]


def shards(integrals, coefficients, pair_list, partial_owner, partial_slot):
    na, no = lax.axis_size("aux"), lax.axis_size("orb")
    per, bs, nocc = coefficients.shape
    lmb = pair_list.shape[0] // 4
    naux = integrals.shape[2] // bs
    mp = bs // na // 2
    width = na * 16
    rows = na * no
    el = mp * 128
    dims = (na, no, lmb, bs, nocc, naux, per)
    dma = pltpu.SemaphoreType.DMA
    vmem = pltpu.VMEM
    any_spec = pl.BlockSpec(memory_space=pltpu.HBM)
    return pl.pallas_call(
        functools.partial(kernel, dims),
        out_shape=jax.ShapeDtypeStruct((1, bs * bs), F32),
        in_specs=[any_spec] * 5,
        out_specs=pl.BlockSpec(memory_space=pltpu.VMEM),
        scratch_shapes=[
            pltpu.SMEM(pair_list.shape, I32),
            pltpu.SMEM(partial_slot.shape, I32),
            pltpu.SMEM(partial_slot.shape, I32),
            vmem(integrals.shape, BF16),
            vmem(coefficients.shape, BF16),
            vmem((per, 16, 128), BF16),
            vmem((no * per, 8, 128), BF16),
            vmem((no * per, 8, 128), BF16),
            vmem((na, 8, width), I32),
            pltpu.SMEM((na, 8, min(width, 128)), I32),
            vmem((2, na, lmb, 16, 128), BF16),
            vmem((lmb, 2 * bs, nocc), BF16),
            vmem((2, na, lmb, 16, 128), BF16),
            vmem((lmb, bs * naux, 4 * bs), BF16),
            vmem((lmb * bs, naux * nocc), BF16),
            vmem((lmb // 2, bs * 8, 128), F32),
            vmem((na, mp, 16, lmb * bs), BF16),
            vmem((na, mp, 16, lmb * bs), BF16),
            vmem((4 * rows, lmb // 2 * width), BF16),
            vmem((no, na, el), BF16),
            vmem((no, na, el), BF16),
            vmem((na, 1, el), F32),
            vmem((na, 1, el), F32),
            dma((7,)),
            dma((10,)),
            dma((10,)),
        ],
        compiler_params=pltpu.CompilerParams(
            collective_id=0, has_side_effects=True, vmem_limit_bytes=60 * 2**20
        ),
    )(integrals, coefficients, pair_list, partial_owner.reshape(-1), partial_slot)


def solution(mesh):
    in_specs = (
        P(("aux", "orb"), None, None),
        P("orb", None, None),
        P(("aux", "orb")),
        P(("aux", "orb"), None),
        P(("aux", "orb")),
    )
    out_specs = P(("aux", "orb"), None)
    return jax.shard_map(shards, mesh=mesh, in_specs=in_specs, out_specs=out_specs, check_vma=False)
```

time: 372 us -> 51.8 us (0.14)
  waiting for transfers between devices: 337 us -> 0 us
  Pallas kernels: 0 us -> 50.3 us
  between operations: 13.4 us -> 0.01 us
  local copies, waits for them, and re-layouts: 10.6 us -> 1.32 us
  matrix products: 5.55 us -> 0 us
  other arithmetic: 4.74 us -> 0 us
    unnamed x3 -> x0, waiting for transfers between devices: 266 us -> none
    all_gather x1 -> x0, waiting for transfers between devices: 70.6 us -> none  [shards(): everything = lax.all_gather(coefficients, 'orb', axis=0, tiled=True)]
    pallas_call x0 -> x1, Pallas kernels: none -> 50.3 us  [shards(): pl.pallas_call(functools.partial(kernel, dims), out_shape=jax.ShapeDtypeS...]
    gather x3 -> x0, local copies, waits for them, and re-layouts: 6.86 us -> none  [the longest x1 5.83 us: shards(): everything[pair_list].reshape(slot_count, 4 * block_size, occ_width)]
    dot_general x2 -> x0, matrix products: 5.55 us -> none  [the longest x1 3.52 us: shards(): jnp.einsum('smpi,tnpi->stmn', halfway, halfway, preferred_element_type=jn...]
  transfers between devices with their start and end apart: 2 -> 0, of which waited for: 2 -> 0; matrix products, arithmetic and copies ran while one was open for 0% -> 0% of each run, Pallas kernels for 0% -> 0%
where the time goes in v2:
time: 51.8 us; the launch traced here: 51.6 us
  Pallas kernels  50.3 us (97%)
  local copies, waits for them, and re-layouts  1.32 us (3%)
    pallas_call x1, Pallas kernels, shards(): pl.pallas_call(functools.partial(kernel, dims), out_shape=jax.ShapeDtypeS...  50.3 us
    unnamed x1, local copies, waits for them, and re-layouts  1.32 us

profile of v2, /device:TPU:1, one launch (start us, length us, event | category | flops | bytes accessed | tf_op | source)
XLA Modules:
  0.0 51.6 jit_solution(1387674630212878798)
XLA Ops:
  0.0 50.3 %shard_map.55 = f32[1,4096]{1,0:T(1,128)} custom-call(bf16[24,64,256]{2,1,0:T(8,128)(2,1)} %ints_ref.1, bf16[10,64,512]{2,1,0:T(8,128)(2,1)} %coef_ref.1, s32[24]{0:T(128)} %pairs_hbm.1, s32[30]{0:T(128)} %bitcast.1, s32[30]{0:T(128)} %slot_hbm.1), custom_call_target="tpu_custom_call" | custom-call | tf_op jit(solution)/shard_map/pallas_call | solution.py:326
  50.3 1.3 %copy.7 = f32[1,4096]{1,0:T(1,128)} copy(f32[1,4096]{1,0:T(1,128)} %shard_map.55) | data formatting | bytes 32768

commit v3 on v2

--- a/solution.py
+++ b/solution.py
@@ -10,6 +10,19 @@
 
 MESH = pl.DeviceIdType.MESH
 F32, BF16, I32 = jnp.float32, jnp.bfloat16, jnp.int32
+
+
+def block_places(lmb):
+    chunks = (lmb - 2) // 2
+    places = [[[None, None] for _ in range(8)] for _ in range(chunks)]
+    for chunk in range(chunks):
+        for s in range(lmb):
+            for h in range(2):
+                places[chunk][s][h] = (s, (s + 2 * chunk + 1 + h) % lmb)
+    for s in range(lmb):
+        row, h = divmod(s, 2)
+        places[row // 2][lmb + row % 2][h] = (s, (s + lmb - 1) % lmb)
+    return places
 
 
 def kernel(
@@ -29,6 +42,7 @@
     zbuf_a,
     zbuf_b,
     msgs,
+    asked,
     idsm,
     packed,
     near,
@@ -52,7 +66,8 @@
     nz = no // 2
     nic = nocc // 128
     mp = bs // na // 2
-    half = lmb // 2
+    chunks = (lmb - 2) // 2
+    places = block_places(lmb)
     width = na * 16
     rows = na * no
     el = mp * 128
@@ -111,7 +126,8 @@
     def all_of(part, stage):
         return remote(part, part, stage, (a, sib))
 
-    za, zb, wa, wb, ids_at, pa, pb, xs, ds, fs = range(10)
+    za, zb, wa, wb, ids_at, pa, pb, fs, xs = range(9)
+    ds = xs + mp
 
     load_t.wait()
     zbuf_a[own] = tiles[:, 0:8, :]
@@ -122,16 +138,19 @@
     row_at = lax.broadcasted_iota(I32, (8, width), 0)
     lane_at = lax.broadcasted_iota(I32, (8, width), 1)
     note = jnp.zeros((8, width), I32)
-    for s in range(lmb):
-        for t in range(lmb):
-            if s != t:
-                j = s * (lmb - 1) + t - (1 if t > s else 0)
-                place = slot_ref[j] * na + owner_ref[j] + 1
-                here = (row_at == t) & ((lane_at == a * 16 + s) | (lane_at == a * 16 + 8 + s))
-                note = jnp.where(here, place, note)
-    for j in range(4 * lmb):
-        if j % 4 >= 2:
-            note = jnp.where((row_at == lmb) & (lane_at == j), pairs_ref[j], note)
+    for chunk in range(chunks):
+        for h in range(2):
+            for u in range(8):
+                if places[chunk][u][h] is not None:
+                    s, t = places[chunk][u][h]
+                    j = s * (lmb - 1) + t - (1 if t > s else 0)
+                    place = slot_ref[j] * na + owner_ref[j] + 1
+                    here = (row_at == 2 * chunk + h) & ((lane_at == a * 16 + u) | (lane_at == a * 16 + 8 + u))
+                    note = jnp.where(here, place, note)
+    for s in range(lmb):
+        for k in range(2):
+            here = (row_at == 2 * chunks) & (lane_at == a * 16 + 2 * s + k)
+            note = jnp.where(here, pairs_ref[4 * s + 2 + k], note)
     msgs[a] = note
 
     pl.semaphore_wait(barrier, na + no - 2)
@@ -147,7 +166,6 @@
         return 0
 
     lax.fori_loop(0, na - 1, start_ids, 0)
-    start_z(1, zb)
 
     load_g.wait()
     height = bs * naux
@@ -162,30 +180,33 @@
         turned = lax.dot_general(turn, block, (((1,), (1,)), ((), ())), preferred_element_type=F32).astype(BF16)
         gt[s] = jnp.dot(turned, order, preferred_element_type=F32).astype(BF16)
 
-    load_c.wait()
-    for s in range(lmb):
-        for k in range(2):
-            near[s, pl.ds(k * bs, bs), :] = cbuf[lax.rem(pairs_ref[4 * s + k], per)]
-    xbuf[...] = jnp.zeros_like(xbuf)
-
-    all_of(msgs.at[pl.ds(0, na - 1)], ids_at).wait_recv()
-    to_scalar = pltpu.make_async_copy(msgs.at[:, :, pl.ds(0, min(width, 128))], idsm, load_sem.at[3])
-    to_scalar.start()
-
-    ids = msgs[0]
-    for src in range(1, na):
-        ids = ids + msgs[src]
-    to_scalar.wait()
-
     def swap(h, z_stage, w_stage):
         all_of(zbuf[h].at[pl.ds(0, (nz - 1) * per)], z_stage).wait_recv()
         for i in range(nz):
             part = zbuf[h].at[pl.ds((2 * i + c) * per, per)]
             remote(part, part, w_stage, (a, sib)).start()
 
+    start_z(1, zb)
+
+    load_c.wait()
+    for s in range(lmb):
+        for k in range(2):
+            near[s, pl.ds(k * bs, bs), :] = cbuf[lax.rem(pairs_ref[4 * s + k], per)]
+    xbuf[...] = jnp.zeros_like(xbuf)
+
+    all_of(msgs.at[pl.ds(0, na - 1)], ids_at).wait_recv()
+    ids = msgs[0]
+    for src in range(1, na):
+        ids = ids + msgs[src]
+    asked[...] = ids[2 * chunks : 2 * chunks + 1, :]
+    to_scalar = pltpu.make_async_copy(asked, idsm, load_sem.at[3])
+    to_scalar.start()
+    swap(0, za, wa)
+    to_scalar.wait()
+
     def pair(h, to, s):
         return jnp.concatenate(
-            [zbuf[h][idsm[to, lmb, 4 * s + 2]], zbuf[h][idsm[to, lmb, 4 * s + 3]]], axis=0
+            [zbuf[h][idsm[0, to * 16 + 2 * s + k]] for k in range(2)], axis=0
         )
 
     def exchange(h, w_stage, p_stage):
@@ -202,7 +223,6 @@
         for s in range(lmb):
             far[h, a, s] = pair(h, a, s)
 
-    swap(0, za, wa)
     exchange(0, wa, pa)
     swap(1, zb, wb)
     exchange(1, wb, pb)
@@ -210,7 +230,7 @@
     r_at = lax.broadcasted_iota(I32, (rows, width), 0) + 1
     l_at = (lax.broadcasted_iota(I32, (rows, width), 1) // 8) % 2
     for h in range(2):
-        for tp in range(half):
+        for tp in range(chunks):
             hit = r_at == ids[2 * tp + h : 2 * tp + h + 1, :]
             for m2 in range(2):
                 onehot[pl.ds((m2 * 2 + h) * rows, rows), pl.ds(tp * width, width)] = (
@@ -232,62 +252,64 @@
 
     whole = hcat[...]
     products = lax.dot_general(whole, whole, (((1,), (1,)), ((), ())), preferred_element_type=F32)
-    for s in range(lmb):
-        for tp in range(half):
-            xbuf[tp, pl.ds(s, bs, stride=8), :] = products[s * bs : (s + 1) * bs, tp * 128 : (tp + 1) * 128]
+    left = lax.broadcasted_iota(I32, (bs, 128), 1) < bs
+
+    def block_half(place, h):
+        s, t = place
+        tile = products[s * bs : (s + 1) * bs, t // 2 * 128 : t // 2 * 128 + 128]
+        return tile if t % 2 == h else pltpu.roll(tile, 64, 1)
+
+    for chunk in range(chunks):
+        for u in range(8):
+            first, second = places[chunk][u]
+            if first is not None:
+                value = jnp.where(left, block_half(first, 0), block_half(second, 1))
+                xbuf[chunk, pl.ds(u, bs, stride=8), :] = value
 
     def x_rows(e, q):
         at = pl.ds(pl.multiple_of((e * mp + q) * 16, 16), 16)
-        return jnp.concatenate([xbuf[tp, at, :] for tp in range(half)], axis=1).astype(BF16)
-
-    def send_x(i, _):
-        to = plane_peer(i)
-        for q in range(mp):
-            xsend[to, q] = x_rows(to, q)
-        remote(xsend.at[to], xrecv.at[a], xs, (to, o)).start()
-        return 0
-
-    lax.fori_loop(0, na - 1, send_x, 0)
-    for q in range(mp):
-        xrecv[a, q] = x_rows(a, q)
-    all_of(xrecv.at[pl.ds(0, na - 1)], xs).wait_recv()
-
-    right = [
-        jnp.concatenate(
-            [xrecv[:, q, :, pl.ds(tp * 128, 128)].reshape(width, 128) for q in range(mp)], axis=1
-        )
-        for tp in range(half)
-    ]
-
-    def product(block):
-        total = None
-        for tp in range(half):
-            term = jnp.dot(
-                onehot[pl.ds(block * rows, rows), pl.ds(tp * width, width)], right[tp], preferred_element_type=F32
-            )
-            total = term if total is None else total + term
-        return total
-
-    z00, z01, z10, z11 = product(0), product(1), product(2), product(3)
+        return jnp.concatenate([xbuf[tp, at, :] for tp in range(chunks)], axis=1).astype(BF16)
+
+    def send_x(q):
+        def send(i, _):
+            to = plane_peer(i)
+            xsend[q, to] = x_rows(to, q)
+            remote(xsend.at[q, to], xrecv.at[q, a], xs + q, (to, o)).start()
+            return 0
+
+        lax.fori_loop(0, na - 1, send, 0)
+
+    for q in range(mp):
+        send_x(q)
+    for q in range(mp):
+        xrecv[q, a] = x_rows(a, q)
+
     low = lax.broadcasted_iota(I32, (rows, 128), 1) < 64
-    for q in range(mp):
-        at = slice(q * 128, (q + 1) * 128)
-        first = z00[:, at] + pltpu.roll(z01[:, at], 64, 1)
-        second = pltpu.roll(z10[:, at], 64, 1) + z11[:, at]
-        dense = jnp.where(low, first, second).astype(BF16)
-        dsend[:, :, pl.ds(q * 128, 128)] = dense.reshape(no, na, 128)
-
-    for i in o_order:
-        to = (o + i) % no
-        remote(dsend.at[to], drecv.at[o], ds, (a, to)).start()
-    drecv[o] = dsend[o]
-    all_of(drecv.at[pl.ds(0, no - 1)], ds).wait_recv()
-
-    total = drecv[0].astype(F32)
-    for src in range(1, no):
-        total = total + drecv[src].astype(F32)
-    for r in range(na):
-        fsend[r] = total[r : r + 1, :]
+
+    def send_d(q):
+        all_of(xrecv.at[q, pl.ds(0, na - 1)], xs + q).wait_recv()
+        right = [xrecv[q, :, :, pl.ds(tp * 128, 128)].reshape(width, 128) for tp in range(chunks)]
+        right = jnp.concatenate(right, axis=0)
+        z00, z01, z10, z11 = [
+            jnp.dot(onehot[pl.ds(block * rows, rows), :], right, preferred_element_type=F32) for block in range(4)
+        ]
+        first = z00 + pltpu.roll(z01, 64, 1)
+        second = pltpu.roll(z10, 64, 1) + z11
+        dsend[q] = jnp.where(low, first, second).astype(BF16).reshape(no, na, 128)
+        for i in o_order:
+            to = (o + i) % no
+            remote(dsend.at[q, to], drecv.at[q, o], ds + q, (a, to)).start()
+        drecv[q, o] = dsend[q, o]
+
+    for q in range(mp):
+        send_d(q)
+    for q in range(mp):
+        all_of(drecv.at[q, pl.ds(0, no - 1)], ds + q).wait_recv()
+        total = drecv[q, 0].astype(F32)
+        for src in range(1, no):
+            total = total + drecv[q, src].astype(F32)
+        for r in range(na):
+            fsend[r, :, pl.ds(q * 128, 128)] = total[r : r + 1, :]
 
     def send_f(i, _):
         to = plane_peer(i)
@@ -302,8 +324,9 @@
         all_of(zbuf[h].at[pl.ds(0, nz * per)], w_stage).wait_send()
         all_of(packed.at[h, pl.ds(0, na - 1)], p_stage).wait_send()
     all_of(msgs.at[pl.ds(0, na - 1)], ids_at).wait_send()
-    all_of(xsend.at[pl.ds(0, na - 1)], xs).wait_send()
-    all_of(dsend.at[pl.ds(0, no - 1)], ds).wait_send()
+    for q in range(mp):
+        all_of(xsend.at[q, pl.ds(0, na - 1)], xs + q).wait_send()
+        all_of(dsend.at[q, pl.ds(0, no - 1)], ds + q).wait_send()
     all_of(frecv.at[pl.ds(0, na - 1)], fs).wait_recv()
     all_of(fsend.at[pl.ds(0, na - 1)], fs).wait_send()
     for e in range(na):
@@ -319,6 +342,7 @@
     width = na * 16
     rows = na * no
     el = mp * 128
+    chunks = (lmb - 2) // 2
     dims = (na, no, lmb, bs, nocc, naux, per)
     dma = pltpu.SemaphoreType.DMA
     vmem = pltpu.VMEM
@@ -338,23 +362,24 @@
             vmem((no * per, 8, 128), BF16),
             vmem((no * per, 8, 128), BF16),
             vmem((na, 8, width), I32),
-            pltpu.SMEM((na, 8, min(width, 128)), I32),
+            vmem((1, width), I32),
+            pltpu.SMEM((1, width), I32),
             vmem((2, na, lmb, 16, 128), BF16),
             vmem((lmb, 2 * bs, nocc), BF16),
             vmem((2, na, lmb, 16, 128), BF16),
             vmem((lmb, bs * naux, 4 * bs), BF16),
             vmem((lmb * bs, naux * nocc), BF16),
-            vmem((lmb // 2, bs * 8, 128), F32),
-            vmem((na, mp, 16, lmb * bs), BF16),
-            vmem((na, mp, 16, lmb * bs), BF16),
-            vmem((4 * rows, lmb // 2 * width), BF16),
-            vmem((no, na, el), BF16),
-            vmem((no, na, el), BF16),
+            vmem((chunks, bs * 8, 128), F32),
+            vmem((mp, na, 16, chunks * 128), BF16),
+            vmem((mp, na, 16, chunks * 128), BF16),
+            vmem((4 * rows, chunks * width), BF16),
+            vmem((mp, no, na, 128), BF16),
+            vmem((mp, no, na, 128), BF16),
             vmem((na, 1, el), F32),
             vmem((na, 1, el), F32),
             dma((7,)),
-            dma((10,)),
-            dma((10,)),
+            dma((8 + 2 * mp,)),
+            dma((8 + 2 * mp,)),
         ],
         compiler_params=pltpu.CompilerParams(
             collective_id=0, has_side_effects=True, vmem_limit_bytes=60 * 2**20

time: 51.8 us -> 50 us (0.965)
  Pallas kernels: 50.3 us -> 48.5 us
    pallas_call x1, Pallas kernels: 50.3 us -> 48.5 us  [shards(): pl.pallas_call(functools.partial(kernel, dims), out_shape=jax.ShapeDtypeS...]
where the time goes in v3:
time: 50 us; the launch traced here: 49.9 us
  Pallas kernels  48.5 us (97%)
  local copies, waits for them, and re-layouts  1.32 us (3%)
    pallas_call x1, Pallas kernels, shards(): pl.pallas_call(functools.partial(kernel, dims), out_shape=jax.ShapeDtypeS...  48.5 us
    unnamed x1, local copies, waits for them, and re-layouts  1.32 us

profile of v3, /device:TPU:1, one launch (start us, length us, event | category | flops | bytes accessed | tf_op | source)
XLA Modules:
  0.0 49.9 jit_solution(3905218644514813522)
XLA Ops:
  0.0 48.5 %shard_map.55 = f32[1,4096]{1,0:T(1,128)} custom-call(bf16[24,64,256]{2,1,0:T(8,128)(2,1)} %ints_ref.1, bf16[10,64,512]{2,1,0:T(8,128)(2,1)} %coef_ref.1, s32[24]{0:T(128)} %pairs_hbm.1, s32[30]{0:T(128)} %bitcast.1, s32[30]{0:T(128)} %slot_hbm.1), custom_call_target="tpu_custom_call" | custom-call | tf_op jit(solution)/shard_map/pallas_call | solution.py:350
  48.5 1.3 %copy.7 = f32[1,4096]{1,0:T(1,128)} copy(f32[1,4096]{1,0:T(1,128)} %shard_map.55) | data formatting | bytes 32768

commit v4 on v3

--- a/solution.py
+++ b/solution.py
@@ -10,6 +10,16 @@
 
 MESH = pl.DeviceIdType.MESH
 F32, BF16, I32 = jnp.float32, jnp.bfloat16, jnp.int32
+
+
+def holders(side):
+    def distance(at):
+        return sum(abs(d) for d in at)
+
+    offsets = range(-((side - 1) // 2), side // 2 + 1)
+    plane = [(dx, dy) for dx in offsets for dy in offsets if 0 < distance((dx, dy)) and 2 * distance((dx, dy)) <= side + 1]
+    reach = [(dx, dy) for dx in offsets for dy in offsets if 2 * (side - distance((dx, dy))) > side + 1]
+    return plane, [(dx, dy, 1 if dx + dy >= 0 else -1) for dx, dy in reach]
 
 
 def block_places(lmb):
@@ -39,9 +49,11 @@
     gbuf,
     cbuf,
     tiles,
+    zalt,
     zbuf_a,
     zbuf_b,
     msgs,
+    crossmsgs,
     asked,
     idsm,
     packed,
@@ -49,6 +61,7 @@
     far,
     gt,
     hcat,
+    xhalf,
     xbuf,
     xsend,
     xrecv,
@@ -76,8 +89,16 @@
     x, y = a // side, a % side
     z, c = o // 2, o % 2
     sib = o + 1 - 2 * c
-    lg = pl.multiple_of((a // nic) * 16, 16)
-    lane0 = pl.multiple_of((a % nic) * 128, 128)
+    piece = bs * nic // 2 // na
+    groups = bs // piece
+    near_by, crossed = holders(side)
+
+    def plane_at(dx, dy):
+        return ((x + dx) % side) * side + (y + dy) % side
+
+    turned = (side // 2) * (z % 2)
+    tile = plane_at(turned, turned)
+    held = (tile, plane_at(side // 2 - turned, side // 2 - turned))
     own = pl.ds(o * per, per)
     zbuf = (zbuf_a, zbuf_b)
 
@@ -98,8 +119,24 @@
         return 0
 
     lax.fori_loop(0, na - 1, greet, 0)
-
-    load_t = pltpu.make_async_copy(coef_ref.at[:, pl.ds(lg, 16), pl.ds(lane0, 128)], tiles, load_sem.at[2])
+    extra = [at for at in crossed if at[:2] != (0, 0)]
+    for dx, dy, dz in extra:
+        there = (plane_at(dx, dy), ((z + dz) % nz) * 2 + c)
+        pl.semaphore_signal(barrier, inc=1, device_id=there, device_id_type=MESH)
+
+    load_t = [
+        pltpu.make_async_copy(
+            coef_ref.at[
+                :,
+                pl.ds(pl.multiple_of(held[v] % groups * piece // 16 * 16, 16), 16),
+                pl.ds(pl.multiple_of((h * nic // 2 + held[v] // groups) * 128, 128), 128),
+            ],
+            tiles.at[v, h],
+            load_sem.at[8 + 2 * v + h],
+        )
+        for v in range(2)
+        for h in range(2)
+    ]
     load_c = pltpu.make_async_copy(coef_ref, cbuf, load_sem.at[0])
     load_g = pltpu.make_async_copy(ints_ref, gbuf, load_sem.at[1])
     scalars = [
@@ -107,7 +144,8 @@
         pltpu.make_async_copy(owner_hbm, owner_ref, load_sem.at[5]),
         pltpu.make_async_copy(slot_hbm, slot_ref, load_sem.at[6]),
     ]
-    load_t.start()
+    for copy in load_t:
+        copy.start()
     for copy in scalars:
         copy.start()
     load_c.start()
@@ -126,12 +164,20 @@
     def all_of(part, stage):
         return remote(part, part, stage, (a, sib))
 
-    za, zb, wa, wb, ids_at, pa, pb, fs, xs = range(9)
+    za, zb, wa, wb, ids_at, cross_at, pa, pb, fs, xs = range(10)
     ds = xs + mp
 
-    load_t.wait()
-    zbuf_a[own] = tiles[:, 0:8, :]
-    zbuf_b[own] = tiles[:, 8:16, :]
+    for v in range(2):
+        for h in range(2):
+            load_t[2 * v + h].wait()
+            part = tiles[v, h]
+            if piece < 16:
+                part = jnp.where(held[v] % groups % 2 == 0, part[:, :piece], part[:, piece:])
+            if v == 0:
+                zbuf[h][own] = part
+            else:
+                zalt[h] = part
+
     for copy in scalars:
         copy.wait()
 
@@ -153,11 +199,12 @@
             note = jnp.where(here, pairs_ref[4 * s + 2 + k], note)
     msgs[a] = note
 
-    pl.semaphore_wait(barrier, na + no - 2)
+    pl.semaphore_wait(barrier, na + no - 2 + len(extra))
 
     def start_z(h, stage):
         for i in z_order:
-            remote(zbuf[h].at[own], zbuf[h].at[own], stage, (a, ((z + i) % nz) * 2 + c)).start()
+            source = zbuf[h].at[own] if i % 2 == 0 else zalt.at[h]
+            remote(source, zbuf[h].at[own], stage, (a, ((z + i) % nz) * 2 + c)).start()
 
     start_z(0, za)
 
@@ -165,6 +212,9 @@
         remote(msgs.at[a], msgs.at[a], ids_at, (plane_peer(i), o)).start()
         return 0
 
+    for n, (dx, dy, dz) in enumerate(crossed):
+        there = (plane_at(dx, dy), ((z + dz) % nz) * 2 + c)
+        remote(msgs.at[a], crossmsgs.at[n], cross_at, there).start()
     lax.fori_loop(0, na - 1, start_ids, 0)
 
     load_g.wait()
@@ -173,7 +223,7 @@
     c_at = lax.broadcasted_iota(I32, (height, height), 1)
     turn = (c_at == (r_at % bs) * naux + r_at // bs).astype(F32).astype(BF16)
     j = c_at - 2 * bs
-    source = 2 * bs + (j // 8 % 2) * bs + (j // 16 % (bs // 16)) * 16 + (j // bs) * 8 + j % 8
+    source = 2 * bs + (j // piece % 2) * bs + (j // (2 * piece)) * piece + j % piece
     order = (r_at == jnp.where(c_at < 2 * bs, c_at, source)).astype(F32).astype(BF16)
     for s in range(lmb):
         block = gbuf[4 * s : 4 * s + 4].reshape(4 * bs, height)
@@ -198,30 +248,31 @@
     ids = msgs[0]
     for src in range(1, na):
         ids = ids + msgs[src]
-    asked[...] = ids[2 * chunks : 2 * chunks + 1, :]
+    asked[0:1, :] = ids[2 * chunks : 2 * chunks + 1, :]
+    all_of(crossmsgs, cross_at).wait_recv()
+    others = crossmsgs[0]
+    for n in range(1, len(crossed)):
+        others = others + crossmsgs[n]
+    asked[1:2, :] = others[2 * chunks : 2 * chunks + 1, :]
     to_scalar = pltpu.make_async_copy(asked, idsm, load_sem.at[3])
     to_scalar.start()
     swap(0, za, wa)
     to_scalar.wait()
 
-    def pair(h, to, s):
-        return jnp.concatenate(
-            [zbuf[h][idsm[0, to * 16 + 2 * s + k]] for k in range(2)], axis=0
-        )
+    def pair(h, row, asker, s):
+        return jnp.concatenate([zbuf[h][idsm[row, asker * 16 + 2 * s + k]] for k in range(2)], axis=0)
 
     def exchange(h, w_stage, p_stage):
         all_of(zbuf[h].at[pl.ds(0, nz * per)], w_stage).wait_recv()
-
-        def pack(i, _):
-            to = plane_peer(i)
+        served = [(0, plane_at(dx, dy), o) for dx, dy in near_by if abs(dx) + abs(dy) > 1]
+        served += [(1, plane_at(-dx, -dy), ((z - dz) % nz) * 2 + c) for dx, dy, dz in crossed]
+        served += [(0, plane_at(dx, dy), o) for dx, dy in near_by if abs(dx) + abs(dy) == 1]
+        for n, (row, asker, orb) in enumerate(served):
             for s in range(lmb):
-                packed[h, to, s] = pair(h, to, s)
-            remote(packed.at[h, to], far.at[h, a], p_stage, (to, o)).start()
-            return 0
-
-        lax.fori_loop(0, na - 1, pack, 0)
+                packed[h, n, s] = pair(h, row, asker, s)
+            remote(packed.at[h, n], far.at[h, tile], p_stage, (asker, orb)).start()
         for s in range(lmb):
-            far[h, a, s] = pair(h, a, s)
+            far[h, tile, s] = pair(h, 0, a, s)
 
     exchange(0, wa, pa)
     swap(1, zb, wb)
@@ -237,21 +288,23 @@
                     jnp.where(hit & (l_at == m2), 1.0, 0.0).astype(BF16)
                 )
 
-    all_of(far.at[0, pl.ds(0, na - 1)], pa).wait_recv()
-    all_of(far.at[1, pl.ds(0, na - 1)], pb).wait_recv()
-
-    for s in range(lmb):
-        there = [
-            jnp.concatenate([far[h, g * nic + i, s] for h in range(2) for g in range(bs // 16)], axis=0)
-            for i in range(nic)
-        ]
-        block = jnp.concatenate([near[s], jnp.concatenate(there, axis=1)], axis=0)
-        halfway = jnp.dot(gt[s], block, preferred_element_type=F32).astype(BF16)
-        for p in range(naux):
-            hcat[pl.ds(s * bs, bs), pl.ds(p * nocc, nocc)] = halfway[p * bs : (p + 1) * bs]
-
-    whole = hcat[...]
-    products = lax.dot_general(whole, whole, (((1,), (1,)), ((), ())), preferred_element_type=F32)
+    def multiply(h, p_stage):
+        all_of(far.at[h, pl.ds(0, na - 1)], p_stage).wait_recv()
+        wide = nocc // 2
+        for s in range(lmb):
+            there = [
+                jnp.concatenate([far[h, i * groups + g, s] for g in range(groups)], axis=0) for i in range(nic // 2)
+            ]
+            there = jnp.concatenate(there, axis=1) if nic > 2 else there[0]
+            block = jnp.concatenate([near[s, :, pl.ds(h * wide, wide)], there], axis=0)
+            halfway = jnp.dot(gt[s], block, preferred_element_type=F32).astype(BF16)
+            for p in range(naux):
+                hcat[h, pl.ds(s * bs, bs), pl.ds(p * wide, wide)] = halfway[p * bs : (p + 1) * bs]
+        whole = hcat[h]
+        return lax.dot_general(whole, whole, (((1,), (1,)), ((), ())), preferred_element_type=F32)
+
+    xhalf[...] = multiply(0, pa)
+    products = xhalf[...] + multiply(1, pb)
     left = lax.broadcasted_iota(I32, (bs, 128), 1) < bs
 
     def block_half(place, h):
@@ -324,6 +377,7 @@
         all_of(zbuf[h].at[pl.ds(0, nz * per)], w_stage).wait_send()
         all_of(packed.at[h, pl.ds(0, na - 1)], p_stage).wait_send()
     all_of(msgs.at[pl.ds(0, na - 1)], ids_at).wait_send()
+    all_of(crossmsgs, cross_at).wait_send()
     for q in range(mp):
         all_of(xsend.at[q, pl.ds(0, na - 1)], xs + q).wait_send()
         all_of(dsend.at[q, pl.ds(0, no - 1)], ds + q).wait_send()
@@ -343,6 +397,7 @@
     rows = na * no
     el = mp * 128
     chunks = (lmb - 2) // 2
+    piece = bs * nocc // 256 // na
     dims = (na, no, lmb, bs, nocc, naux, per)
     dma = pltpu.SemaphoreType.DMA
     vmem = pltpu.VMEM
@@ -358,17 +413,20 @@
             pltpu.SMEM(partial_slot.shape, I32),
             vmem(integrals.shape, BF16),
             vmem(coefficients.shape, BF16),
-            vmem((per, 16, 128), BF16),
-            vmem((no * per, 8, 128), BF16),
-            vmem((no * per, 8, 128), BF16),
+            vmem((2, 2, per, 16, 128), BF16),
+            vmem((2, per, piece, 128), BF16),
+            vmem((no * per, piece, 128), BF16),
+            vmem((no * per, piece, 128), BF16),
             vmem((na, 8, width), I32),
-            vmem((1, width), I32),
-            pltpu.SMEM((1, width), I32),
-            vmem((2, na, lmb, 16, 128), BF16),
+            vmem((len(holders(math.isqrt(na))[1]), 8, width), I32),
+            vmem((2, width), I32),
+            pltpu.SMEM((2, width), I32),
+            vmem((2, na, lmb, 2 * piece, 128), BF16),
             vmem((lmb, 2 * bs, nocc), BF16),
-            vmem((2, na, lmb, 16, 128), BF16),
+            vmem((2, na, lmb, 2 * piece, 128), BF16),
             vmem((lmb, bs * naux, 4 * bs), BF16),
-            vmem((lmb * bs, naux * nocc), BF16),
+            vmem((2, lmb * bs, naux * nocc // 2), BF16),
+            vmem((lmb * bs, lmb * bs), F32),
             vmem((chunks, bs * 8, 128), F32),
             vmem((mp, na, 16, chunks * 128), BF16),
             vmem((mp, na, 16, chunks * 128), BF16),
@@ -377,12 +435,12 @@
             vmem((mp, no, na, 128), BF16),
             vmem((na, 1, el), F32),
             vmem((na, 1, el), F32),
-            dma((7,)),
-            dma((8 + 2 * mp,)),
-            dma((8 + 2 * mp,)),
+            dma((12,)),
+            dma((9 + 2 * mp,)),
+            dma((9 + 2 * mp,)),
         ],
         compiler_params=pltpu.CompilerParams(
-            collective_id=0, has_side_effects=True, vmem_limit_bytes=60 * 2**20
+            collective_id=0, has_side_effects=True, vmem_limit_bytes=56098816
         ),
     )(integrals, coefficients, pair_list, partial_owner.reshape(-1), partial_slot)
 

time: 50 us -> 46.9 us (0.938)
  Pallas kernels: 48.5 us -> 45.5 us
    pallas_call x1, Pallas kernels: 48.5 us -> 45.5 us  [shards(): pl.pallas_call(functools.partial(kernel, dims), out_shape=jax.ShapeDtypeS...]
    unnamed x1 -> x7, local copies, waits for them, and re-layouts: 1.32 us -> 1.29 us
where the time goes in v4:
time: 46.9 us; the launch traced here: 46.8 us
  Pallas kernels  45.5 us (97%)
  local copies, waits for them, and re-layouts  1.29 us (3%)
    pallas_call x1, Pallas kernels, shards(): pl.pallas_call(functools.partial(kernel, dims), out_shape=jax.ShapeDtypeS...  45.5 us
    unnamed x7, local copies, waits for them, and re-layouts  1.29 us

profile of v4, /device:TPU:1, one launch (start us, length us, event | category | flops | bytes accessed | tf_op | source)
XLA Modules:
  0.0 46.8 jit_solution(12571575539211862707)
XLA Ops:
  0.0 0.0 copy-start.2
  0.0 0.0 copy-start.1
  0.0 0.0 copy-start
  0.0 0.6 %copy-done.2 = s32[30]{0:T(128)S(1)} copy-done((s32[30]{0:T(128)S(1)}, s32[30]{0:T(128)}, u32[]{:S(2)}) %copy-start.2) | copy-done | bytes 144
  0.7 0.0 copy-done.1
  0.7 0.0 copy-done
  0.7 45.5 %shard_map.55 = f32[1,4096]{1,0:T(1,128)S(1)} custom-call(bf16[24,64,256]{2,1,0:T(8,128)(2,1)} %ints_ref.1, bf16[10,64,512]{2,1,0:T(8,128)(2,1)} %coef_ref.1, s32[24]{0:T(128)S(1)} %copy-done, s32[30]{0:T(128)S(1)} %bitcast.1, s32[30]{0:T(128)S(1)} %copy-done.2), custom_call_target="tpu_custom_call" | custom-call | tf_op jit(solution)/shard_map/pallas_call | solution.py:405
  46.2 0.6 %copy.7 = f32[1,4096]{1,0:T(1,128)} copy(f32[1,4096]{1,0:T(1,128)S(1)} %shard_map.55) | data formatting | bytes 32768
Async XLA Ops:
  0.0 0.7 %copy-start.2 = (s32[30]{0:T(128)S(1)}, s32[30]{0:T(128)}, u32[]{:S(2)}) copy-start(s32[30]{0:T(128)} %slot_hbm.1) | copy-start | bytes 364
  0.0 0.7 %copy-start.1 = (s32[30,1]{0,1:T(1,128)S(1)}, s32[30,1]{0,1:T(1,128)}, u32[]{:S(2)}) copy-start(s32[30,1]{0,1:T(1,128)} %param.8) | copy-start | bytes 364
  0.0 0.7 %copy-start = (s32[24]{0:T(128)S(1)}, s32[24]{0:T(128)}, u32[]{:S(2)}) copy-start(s32[24]{0:T(128)} %pairs_hbm.1) | copy-start | bytes 292

commit v5 on v4

--- a/solution.py
+++ b/solution.py
@@ -53,7 +53,7 @@
     zbuf_a,
     zbuf_b,
     msgs,
-    crossmsgs,
+    crossnote,
     asked,
     idsm,
     packed,
@@ -98,7 +98,15 @@
 
     turned = (side // 2) * (z % 2)
     tile = plane_at(turned, turned)
-    held = (tile, plane_at(side // 2 - turned, side // 2 - turned))
+    shift = side // 2
+    held = (tile, plane_at(shift - turned, shift - turned))
+    opposite = plane_at(shift, shift)
+    served_by = [(plane_at(dx, dy), o, plane_at(dx + turned, dy + turned), a) for dx, dy in near_by if abs(dx) + abs(dy) > 1]
+    served_by += [
+        (plane_at(dx, dy), ((z + dz) % nz) * 2 + c, plane_at(dx + shift - turned, dy + shift - turned), opposite)
+        for dx, dy, dz in crossed
+    ]
+    served_by += [(plane_at(dx, dy), o, plane_at(dx + turned, dy + turned), a) for dx, dy in near_by if abs(dx) + abs(dy) == 1]
     own = pl.ds(o * per, per)
     zbuf = (zbuf_a, zbuf_b)
 
@@ -164,7 +172,7 @@
     def all_of(part, stage):
         return remote(part, part, stage, (a, sib))
 
-    za, zb, wa, wb, ids_at, cross_at, pa, pb, fs, xs = range(10)
+    za, zb, wa, wb, ids_at, pa, pb, fs, xs = range(9)
     ds = xs + mp
 
     for v in range(2):
@@ -198,6 +206,7 @@
             here = (row_at == 2 * chunks) & (lane_at == a * 16 + 2 * s + k)
             note = jnp.where(here, pairs_ref[4 * s + 2 + k], note)
     msgs[a] = note
+    crossnote[...] = pltpu.roll(note, lax.rem(opposite + na - a, na) * 16, 1)
 
     pl.semaphore_wait(barrier, na + no - 2 + len(extra))
 
@@ -208,14 +217,9 @@
 
     start_z(0, za)
 
-    def start_ids(i, _):
-        remote(msgs.at[a], msgs.at[a], ids_at, (plane_peer(i), o)).start()
-        return 0
-
-    for n, (dx, dy, dz) in enumerate(crossed):
-        there = (plane_at(dx, dy), ((z + dz) % nz) * 2 + c)
-        remote(msgs.at[a], crossmsgs.at[n], cross_at, there).start()
-    lax.fori_loop(0, na - 1, start_ids, 0)
+    for there, orb, _, number in served_by:
+        source = crossnote if number is opposite else msgs.at[a]
+        remote(source, msgs.at[number], ids_at, (there, orb)).start()
 
     load_g.wait()
     height = bs * naux
@@ -248,31 +252,28 @@
     ids = msgs[0]
     for src in range(1, na):
         ids = ids + msgs[src]
-    asked[0:1, :] = ids[2 * chunks : 2 * chunks + 1, :]
-    all_of(crossmsgs, cross_at).wait_recv()
-    others = crossmsgs[0]
-    for n in range(1, len(crossed)):
-        others = others + crossmsgs[n]
-    asked[1:2, :] = others[2 * chunks : 2 * chunks + 1, :]
+    asked[...] = ids[2 * chunks : 2 * chunks + 1, :]
     to_scalar = pltpu.make_async_copy(asked, idsm, load_sem.at[3])
     to_scalar.start()
     swap(0, za, wa)
     to_scalar.wait()
 
-    def pair(h, row, asker, s):
-        return jnp.concatenate([zbuf[h][idsm[row, asker * 16 + 2 * s + k]] for k in range(2)], axis=0)
+    def pair(h, number, s):
+        return jnp.concatenate([zbuf[h][idsm[0, number * 16 + 2 * s + k]] for k in range(2)], axis=0)
 
     def exchange(h, w_stage, p_stage):
         all_of(zbuf[h].at[pl.ds(0, nz * per)], w_stage).wait_recv()
-        served = [(0, plane_at(dx, dy), o) for dx, dy in near_by if abs(dx) + abs(dy) > 1]
-        served += [(1, plane_at(-dx, -dy), ((z - dz) % nz) * 2 + c) for dx, dy, dz in crossed]
-        served += [(0, plane_at(dx, dy), o) for dx, dy in near_by if abs(dx) + abs(dy) == 1]
-        for n, (row, asker, orb) in enumerate(served):
+        served = [(plane_at(dx, dy), plane_at(dx, dy), o) for dx, dy in near_by if abs(dx) + abs(dy) > 1]
+        served += [
+            (plane_at(shift - dx, shift - dy), plane_at(-dx, -dy), ((z - dz) % nz) * 2 + c) for dx, dy, dz in crossed
+        ]
+        served += [(plane_at(dx, dy), plane_at(dx, dy), o) for dx, dy in near_by if abs(dx) + abs(dy) == 1]
+        for n, (number, asker, orb) in enumerate(served):
             for s in range(lmb):
-                packed[h, n, s] = pair(h, row, asker, s)
+                packed[h, n, s] = pair(h, number, s)
             remote(packed.at[h, n], far.at[h, tile], p_stage, (asker, orb)).start()
         for s in range(lmb):
-            far[h, tile, s] = pair(h, 0, a, s)
+            far[h, tile, s] = pair(h, a, s)
 
     exchange(0, wa, pa)
     swap(1, zb, wb)
@@ -323,19 +324,12 @@
         at = pl.ds(pl.multiple_of((e * mp + q) * 16, 16), 16)
         return jnp.concatenate([xbuf[tp, at, :] for tp in range(chunks)], axis=1).astype(BF16)
 
-    def send_x(q):
-        def send(i, _):
-            to = plane_peer(i)
-            xsend[q, to] = x_rows(to, q)
-            remote(xsend.at[q, to], xrecv.at[q, a], xs + q, (to, o)).start()
-            return 0
-
-        lax.fori_loop(0, na - 1, send, 0)
-
     for q in range(mp):
-        send_x(q)
+        for n, (there, orb, e, number) in enumerate(served_by):
+            xsend[q, n] = x_rows(e, q)
+            remote(xsend.at[q, n], xrecv.at[q, number], xs + q, (there, orb)).start()
     for q in range(mp):
-        xrecv[q, a] = x_rows(a, q)
+        xrecv[q, a] = x_rows(tile, q)
 
     low = lax.broadcasted_iota(I32, (rows, 128), 1) < 64
 
@@ -358,11 +352,14 @@
         send_d(q)
     for q in range(mp):
         all_of(drecv.at[q, pl.ds(0, no - 1)], ds + q).wait_recv()
-        total = drecv[q, 0].astype(F32)
-        for src in range(1, no):
-            total = total + drecv[q, src].astype(F32)
-        for r in range(na):
-            fsend[r, :, pl.ds(q * 128, 128)] = total[r : r + 1, :]
+        for v in range(2):
+            total = None
+            for src in range(no):
+                if src // 2 % 2 == v:
+                    term = drecv[q, src].astype(F32)
+                    total = term if total is None else total + term
+            for r in range(na):
+                fsend[r, :, pl.ds(v * el + q * 128, 128)] = total[r : r + 1, :]
 
     def send_f(i, _):
         to = plane_peer(i)
@@ -377,14 +374,14 @@
         all_of(zbuf[h].at[pl.ds(0, nz * per)], w_stage).wait_send()
         all_of(packed.at[h, pl.ds(0, na - 1)], p_stage).wait_send()
     all_of(msgs.at[pl.ds(0, na - 1)], ids_at).wait_send()
-    all_of(crossmsgs, cross_at).wait_send()
     for q in range(mp):
         all_of(xsend.at[q, pl.ds(0, na - 1)], xs + q).wait_send()
         all_of(dsend.at[q, pl.ds(0, no - 1)], ds + q).wait_send()
     all_of(frecv.at[pl.ds(0, na - 1)], fs).wait_recv()
     all_of(fsend.at[pl.ds(0, na - 1)], fs).wait_send()
     for e in range(na):
-        out_ref[:, pl.ds(e * el, el)] = frecv[e]
+        other = (e // side + side // 2) % side * side + (e % side + side // 2) % side
+        out_ref[:, pl.ds(e * el, el)] = frecv[e, :, pl.ds(0, el)] + frecv[other, :, pl.ds(el, el)]
 
 
 def shards(integrals, coefficients, pair_list, partial_owner, partial_slot):
@@ -418,9 +415,9 @@
             vmem((no * per, piece, 128), BF16),
             vmem((no * per, piece, 128), BF16),
             vmem((na, 8, width), I32),
-            vmem((len(holders(math.isqrt(na))[1]), 8, width), I32),
-            vmem((2, width), I32),
-            pltpu.SMEM((2, width), I32),
+            vmem((8, width), I32),
+            vmem((1, width), I32),
+            pltpu.SMEM((1, width), I32),
             vmem((2, na, lmb, 2 * piece, 128), BF16),
             vmem((lmb, 2 * bs, nocc), BF16),
             vmem((2, na, lmb, 2 * piece, 128), BF16),
@@ -433,11 +430,11 @@
             vmem((4 * rows, chunks * width), BF16),
             vmem((mp, no, na, 128), BF16),
             vmem((mp, no, na, 128), BF16),
-            vmem((na, 1, el), F32),
-            vmem((na, 1, el), F32),
+            vmem((na, 1, 2 * el), F32),
+            vmem((na, 1, 2 * el), F32),
             dma((12,)),
-            dma((9 + 2 * mp,)),
-            dma((9 + 2 * mp,)),
+            dma((8 + 2 * mp,)),
+            dma((8 + 2 * mp,)),
         ],
         compiler_params=pltpu.CompilerParams(
             collective_id=0, has_side_effects=True, vmem_limit_bytes=56098816

time: 46.9 us -> 45.4 us (0.968)
  Pallas kernels: 45.5 us -> 44 us
    pallas_call x1, Pallas kernels: 45.5 us -> 44 us  [shards(): pl.pallas_call(functools.partial(kernel, dims), out_shape=jax.ShapeDtypeS...]
where the time goes in v5:
time: 45.4 us; the launch traced here: 45.3 us
  Pallas kernels  44 us (97%)
  local copies, waits for them, and re-layouts  1.29 us (3%)
    pallas_call x1, Pallas kernels, shards(): pl.pallas_call(functools.partial(kernel, dims), out_shape=jax.ShapeDtypeS...  44 us
    unnamed x7, local copies, waits for them, and re-layouts  1.29 us

profile of v5, /device:TPU:1, one launch (start us, length us, event | category | flops | bytes accessed | tf_op | source)
XLA Modules:
  0.0 45.3 jit_solution(17120370328646940071)
XLA Ops:
  0.0 0.0 copy-start.2
  0.0 0.0 copy-start.1
  0.0 0.0 copy-start
  0.0 0.6 %copy-done.2 = s32[30]{0:T(128)S(1)} copy-done((s32[30]{0:T(128)S(1)}, s32[30]{0:T(128)}, u32[]{:S(2)}) %copy-start.2) | copy-done | bytes 144
  0.7 0.0 copy-done.1
  0.7 0.0 copy-done
  0.7 44.0 %shard_map.55 = f32[1,4096]{1,0:T(1,128)S(1)} custom-call(bf16[24,64,256]{2,1,0:T(8,128)(2,1)} %ints_ref.1, bf16[10,64,512]{2,1,0:T(8,128)(2,1)} %coef_ref.1, s32[24]{0:T(128)S(1)} %copy-done, s32[30]{0:T(128)S(1)} %bitcast.1, s32[30]{0:T(128)S(1)} %copy-done.2), custom_call_target="tpu_custom_call" | custom-call | tf_op jit(solution)/shard_map/pallas_call | solution.py:402
  44.7 0.6 %copy.7 = f32[1,4096]{1,0:T(1,128)} copy(f32[1,4096]{1,0:T(1,128)S(1)} %shard_map.55) | data formatting | bytes 32768
Async XLA Ops:
  0.0 0.7 %copy-start.2 = (s32[30]{0:T(128)S(1)}, s32[30]{0:T(128)}, u32[]{:S(2)}) copy-start(s32[30]{0:T(128)} %slot_hbm.1) | copy-start | bytes 364
  0.0 0.7 %copy-start.1 = (s32[30,1]{0,1:T(1,128)S(1)}, s32[30,1]{0,1:T(1,128)}, u32[]{:S(2)}) copy-start(s32[30,1]{0,1:T(1,128)} %param.8) | copy-start | bytes 364
  0.0 0.7 %copy-start = (s32[24]{0:T(128)S(1)}, s32[24]{0:T(128)}, u32[]{:S(2)}) copy-start(s32[24]{0:T(128)} %pairs_hbm.1) | copy-start | bytes 292

commit v6 on v5

--- a/solution.py
+++ b/solution.py
@@ -399,9 +399,11 @@
     dma = pltpu.SemaphoreType.DMA
     vmem = pltpu.VMEM
     any_spec = pl.BlockSpec(memory_space=pltpu.HBM)
+    inputs = (integrals, coefficients, pair_list, partial_owner.reshape(-1), partial_slot)
+    inputs = [pltpu.with_memory_space_constraint(value, pltpu.HBM) for value in inputs]
     return pl.pallas_call(
         functools.partial(kernel, dims),
-        out_shape=jax.ShapeDtypeStruct((1, bs * bs), F32),
+        out_shape=pltpu.VMEM((1, bs * bs), F32),
         in_specs=[any_spec] * 5,
         out_specs=pl.BlockSpec(memory_space=pltpu.VMEM),
         scratch_shapes=[
@@ -437,9 +439,9 @@
             dma((8 + 2 * mp,)),
         ],
         compiler_params=pltpu.CompilerParams(
-            collective_id=0, has_side_effects=True, vmem_limit_bytes=56098816
+            collective_id=0, has_side_effects=True, vmem_limit_bytes=48 * 2**20
         ),
-    )(integrals, coefficients, pair_list, partial_owner.reshape(-1), partial_slot)
+    )(*inputs)
 
 
 def solution(mesh):

time: 45.4 us -> 44.9 us (0.989)
  local copies, waits for them, and re-layouts: 1.29 us -> 0.61 us
    unnamed x7 -> x1, local copies, waits for them, and re-layouts: 1.29 us -> 0.61 us
where the time goes in v6:
time: 44.9 us; the launch traced here: 44.8 us
  Pallas kernels  44.2 us (98%)
  local copies, waits for them, and re-layouts  0.61 us (1%)
    pallas_call x1, Pallas kernels, shards(): pl.pallas_call(functools.partial(kernel, dims), out_shape=pltpu.VMEM((1,...  44.2 us

profile of v6, /device:TPU:1, one launch (start us, length us, event | category | flops | bytes accessed | tf_op | source)
XLA Modules:
  0.0 44.8 jit_solution(3133296993270069891)
XLA Ops:
  0.0 44.2 %shard_map.55 = f32[1,4096]{1,0:T(1,128)S(1)} custom-call(bf16[24,64,256]{2,1,0:T(8,128)(2,1)} %ints_ref.1, bf16[10,64,512]{2,1,0:T(8,128)(2,1)} %coef_ref.1, s32[24]{0:T(128)} %pairs_hbm.1, s32[30]{0:T(128)} %bitcast.1, s32[30]{0:T(128)} %slot_hbm.1), custom_call_target="tpu_custom_call" | custom-call | tf_op jit(solution)/shard_map/pallas_call | solution.py:404
  44.2 0.6 %copy.7 = f32[1,4096]{1,0:T(1,128)} copy(f32[1,4096]{1,0:T(1,128)S(1)} %shard_map.55) | data formatting | bytes 32768

commit v7 on v6

--- a/solution.py
+++ b/solution.py
@@ -126,7 +126,8 @@
         pl.semaphore_signal(barrier, inc=1, device_id=(plane_peer(i), o), device_id_type=MESH)
         return 0
 
-    lax.fori_loop(0, na - 1, greet, 0)
+    for i in range(na - 1):
+        greet(i, 0)
     extra = [at for at in crossed if at[:2] != (0, 0)]
     for dx, dy, dz in extra:
         there = (plane_at(dx, dy), ((z + dz) % nz) * 2 + c)
@@ -186,6 +187,15 @@
             else:
                 zalt[h] = part
 
+    pl.semaphore_wait(barrier, na + no - 2 + len(extra))
+
+    def start_z(h, stage):
+        for i in z_order:
+            source = zbuf[h].at[own] if i % 2 == 0 else zalt.at[h]
+            remote(source, zbuf[h].at[own], stage, (a, ((z + i) % nz) * 2 + c)).start()
+
+    start_z(0, za)
+
     for copy in scalars:
         copy.wait()
 
@@ -208,14 +218,6 @@
     msgs[a] = note
     crossnote[...] = pltpu.roll(note, lax.rem(opposite + na - a, na) * 16, 1)
 
-    pl.semaphore_wait(barrier, na + no - 2 + len(extra))
-
-    def start_z(h, stage):
-        for i in z_order:
-            source = zbuf[h].at[own] if i % 2 == 0 else zalt.at[h]
-            remote(source, zbuf[h].at[own], stage, (a, ((z + i) % nz) * 2 + c)).start()
-
-    start_z(0, za)
 
     for there, orb, _, number in served_by:
         source = crossnote if number is opposite else msgs.at[a]

time: 44.9 us -> 44.7 us (level)
  no operation moved by 1% of the time
where the time goes in v7:
time: 44.7 us; the launch traced here: 44.6 us
  Pallas kernels  44 us (98%)
  local copies, waits for them, and re-layouts  0.61 us (1%)
    pallas_call x1, Pallas kernels, shards(): pl.pallas_call(functools.partial(kernel, dims), out_shape=pltpu.VMEM((1,...  44 us

profile of v7, /device:TPU:1, one launch (start us, length us, event | category | flops | bytes accessed | tf_op | source)
XLA Modules:
  0.0 44.6 jit_solution(3645181676882153081)
XLA Ops:
  0.0 44.0 %shard_map.55 = f32[1,4096]{1,0:T(1,128)S(1)} custom-call(bf16[24,64,256]{2,1,0:T(8,128)(2,1)} %ints_ref.1, bf16[10,64,512]{2,1,0:T(8,128)(2,1)} %coef_ref.1, s32[24]{0:T(128)} %pairs_hbm.1, s32[30]{0:T(128)} %bitcast.1, s32[30]{0:T(128)} %slot_hbm.1), custom_call_target="tpu_custom_call" | custom-call | tf_op jit(solution)/shard_map/pallas_call | solution.py:406
  44.0 0.6 %copy.7 = f32[1,4096]{1,0:T(1,128)} copy(f32[1,4096]{1,0:T(1,128)S(1)} %shard_map.55) | data formatting | bytes 32768

commit v8 on v7

--- a/solution.py
+++ b/solution.py
@@ -141,7 +141,7 @@
                 pl.ds(pl.multiple_of((h * nic // 2 + held[v] // groups) * 128, 128), 128),
             ],
             tiles.at[v, h],
-            load_sem.at[8 + 2 * v + h],
+            load_sem.at[(2, 7, 8, 9)[2 * v + h]],
         )
         for v in range(2)
         for h in range(2)
@@ -265,10 +265,10 @@
 
     def exchange(h, w_stage, p_stage):
         all_of(zbuf[h].at[pl.ds(0, nz * per)], w_stage).wait_recv()
-        served = [(plane_at(dx, dy), plane_at(dx, dy), o) for dx, dy in near_by if abs(dx) + abs(dy) > 1]
-        served += [
+        served = [
             (plane_at(shift - dx, shift - dy), plane_at(-dx, -dy), ((z - dz) % nz) * 2 + c) for dx, dy, dz in crossed
         ]
+        served += [(plane_at(dx, dy), plane_at(dx, dy), o) for dx, dy in near_by if abs(dx) + abs(dy) > 1]
         served += [(plane_at(dx, dy), plane_at(dx, dy), o) for dx, dy in near_by if abs(dx) + abs(dy) == 1]
         for n, (number, asker, orb) in enumerate(served):
             for s in range(lmb):
@@ -436,7 +436,7 @@
             vmem((mp, no, na, 128), BF16),
             vmem((na, 1, 2 * el), F32),
             vmem((na, 1, 2 * el), F32),
-            dma((12,)),
+            dma((10,)),
             dma((8 + 2 * mp,)),
             dma((8 + 2 * mp,)),
         ],

time: 44.7 us -> 44.7 us (level)
  no operation moved by 1% of the time
where the time goes in v8:
time: 44.7 us; the launch traced here: 44.6 us
  Pallas kernels  44 us (98%)
  local copies, waits for them, and re-layouts  0.61 us (1%)
    pallas_call x1, Pallas kernels, shards(): pl.pallas_call(functools.partial(kernel, dims), out_shape=pltpu.VMEM((1,...  44 us

profile of v8, /device:TPU:1, one launch (start us, length us, event | category | flops | bytes accessed | tf_op | source)
XLA Modules:
  0.0 44.6 jit_solution(6516117113877239932)
XLA Ops:
  0.0 44.0 %shard_map.55 = f32[1,4096]{1,0:T(1,128)S(1)} custom-call(bf16[24,64,256]{2,1,0:T(8,128)(2,1)} %ints_ref.1, bf16[10,64,512]{2,1,0:T(8,128)(2,1)} %coef_ref.1, s32[24]{0:T(128)} %pairs_hbm.1, s32[30]{0:T(128)} %bitcast.1, s32[30]{0:T(128)} %slot_hbm.1), custom_call_target="tpu_custom_call" | custom-call | tf_op jit(solution)/shard_map/pallas_call | solution.py:406
  44.0 0.6 %copy.7 = f32[1,4096]{1,0:T(1,128)} copy(f32[1,4096]{1,0:T(1,128)S(1)} %shard_map.55) | data formatting | bytes 32768
